TPU v7x, 32 devices: a whole 2x2x4 slice. The times are simulated.
32 devices in a mesh: blk: 8 (over y, x, core), grp: 4 (over z).
Axes of the slice: x: 2, y: 2, z: 4, core: 2. Of those that a mesh axis runs over, the one named last changes fastest.
Arguments:
- query_rows: bfloat16 [16384, 1024], P(('blk', 'grp')), may hold values from -8 to 8
- key_rows: bfloat16 [16384, 1024], P(('blk', 'grp')), may hold values from -8 to 8
- value_rows: bfloat16 [16384, 1024], P(('blk', 'grp')), may hold values from -6 to 6
- tile_lists: int32 [128, 9], P(('blk', 'grp')), may hold values from -1 to 127, as said below
- hilbert_order: int32 [16384], P(('blk', 'grp')), may hold values from 0 to 16383, as said below
Outputs:
- attention_out: bfloat16 [16384, 1024], P(('blk', 'grp'))
Inputs may be any that keep to these rules, and one draw needn't show every extreme that they name: `tile_lists`: row r lists the key tiles of query tile r. Slot j for j <= 4 holds r - 2 + j or -1; slot 5 + g holds global tile g, the same in every row, the global tiles lying 32 apart. No tile appears twice in a row, and tile r appears in row r. `hilbert_order`: A permutation that maps each aligned block of 512 positions onto itself.
All inputs are finite; a program needn't handle non-finite values.
Results may differ from a plain program's by a relative error of at most 0.0049.
Values may be sent and summed in bfloat16 or wider, within the bound.
No kernel may reach another device: no remote copies, remote signals or barrier semaphores. Data moves between devices by JAX's collectives and lax.ppermute only.
A program may use at most 64 MiB of HBM per device.

v0:
```python
import jax
import jax.numpy as jnp
from jax import lax
from jax.sharding import PartitionSpec as P

LOCAL_HEADS = 8
HEAD_WIDTH = 128
TILE_POINTS = 128
BAND = 2
NG = 4


def extended(block, sides, width):
    for axis, dim in sides:
        count = lax.axis_size(axis)
        forward = [(i, i + 1) for i in range(count - 1)]
        backward = [(target, source) for source, target in forward]
        low = lax.ppermute(
            lax.slice_in_dim(block, block.shape[dim] - width, None, axis=dim), axis, forward
        )
        high = lax.ppermute(lax.slice_in_dim(block, 0, width, axis=dim), axis, backward)
        block = jnp.concatenate([low, block, high], axis=dim)
    return block


def spread(array, axis, root):
    mine = lax.axis_index(axis) == root
    return lax.psum(jnp.where(mine, array, jnp.zeros_like(array)), axis)


def body(query_rows, key_rows, value_rows, tile_lists, hilbert_order):
    row_count = query_rows.shape[0]
    feature_count = query_rows.shape[1]
    tiles_here = row_count // TILE_POINTS
    local_order = hilbert_order % row_count
    q_sorted = query_rows[local_order]
    kv_sorted = jnp.stack([key_rows[local_order], value_rows[local_order]])
    padded = extended(kv_sorted, ((("blk", "grp"), 1),), BAND * TILE_POINTS)
    global_ids = tile_lists[0, 2 * BAND + 1 :]
    fetched = []
    for member in range(NG):
        tile_id = global_ids[member]
        owner_index = tile_id // tiles_here
        start_row = tile_id % tiles_here * TILE_POINTS
        tile_block = lax.dynamic_slice_in_dim(kv_sorted, start_row, TILE_POINTS, 1)
        fetched.append(spread(tile_block, ("blk", "grp"), owner_index))
    global_kv = jnp.concatenate(fetched, axis=1)
    band_valid = tile_lists[:, : 2 * BAND + 1] >= 0
    query_tiles = q_sorted.reshape(tiles_here, TILE_POINTS, LOCAL_HEADS, HEAD_WIDTH)
    global_ok = jnp.ones((NG * TILE_POINTS,), dtype=bool)
    score_scale = HEAD_WIDTH ** (-0.5)

    def one_tile(inputs):
        tile_number, queries_here, valid_here = inputs
        band_kv = lax.dynamic_slice_in_dim(
            padded, tile_number * TILE_POINTS, (2 * BAND + 1) * TILE_POINTS, 1
        )
        kv_here = jnp.concatenate([band_kv, global_kv], axis=1)
        key_heads = kv_here[0].reshape(-1, LOCAL_HEADS, HEAD_WIDTH)
        value_heads = kv_here[1].reshape(-1, LOCAL_HEADS, HEAD_WIDTH)
        allowed = jnp.concatenate([jnp.repeat(valid_here, TILE_POINTS), global_ok])
        scores = (
            jnp.einsum("qhd,khd->hqk", queries_here, key_heads, preferred_element_type=jnp.float32)
            * score_scale
        )
        scores = jnp.where(allowed[None, None, :], scores, -1e30)
        row_peak = jnp.max(scores, axis=-1, keepdims=True)
        exponent = jnp.exp(scores - row_peak)
        weights = (exponent / jnp.sum(exponent, axis=-1, keepdims=True)).astype(jnp.bfloat16)
        attended = jnp.einsum(
            "hqk,khd->qhd", weights, value_heads, preferred_element_type=jnp.float32
        )
        return attended.reshape(TILE_POINTS, feature_count).astype(jnp.bfloat16)

    tile_numbers = jnp.arange(tiles_here, dtype=jnp.int32)
    attended = lax.map(one_tile, (tile_numbers, query_tiles, band_valid)).reshape(
        row_count, feature_count
    )
    return jnp.zeros_like(attended).at[local_order].set(attended)


def solution(mesh):
    in_specs = (
        P(("blk", "grp"), None),
        P(("blk", "grp"), None),
        P(("blk", "grp"), None),
        P(("blk", "grp"), None),
        P(("blk", "grp")),
    )
    out_specs = P(("blk", "grp"), None)
    return jax.shard_map(body, mesh=mesh, in_specs=in_specs, out_specs=out_specs, check_vma=False)
```

profile of v0, /device:TPU:4, one launch (start us, length us, event | category | flops | bytes accessed | tf_op | source)
XLA Modules:
  0.0 347.7 jit_solution(18080044938648163825)
XLA Ops:
  18.9 2.1 gather_fusion
  21.0 2.8 gather_fusion.1
  23.8 3.1 fusion.11
  27.0 2.7 fusion.8
  29.7 3.5 collective-permute-start
  33.2 5.9 %collective-permute-start.1 = (bf16[2,256,1024]{2,1,0:T(8,128)(2,1)}, bf16[2,256,1024]{2,1,0:T(8,128)(2,1)}, u32[]{:S(2)}, u32[]{:S(2)}) collective-permute-start(bf16[2,256,1024]{2,1,0:T(8,128)(2,1)} %get-tuple-element.119), channel_id=1, source_target_pairs={{1,0},{2,1},{3,2},{4,3},{5,4},{6,5},{7,6},{8,7},{9,8},{10,9},{11,1... | collective-permute-start | bytes 3145736 | tf_op jit(solution)/shard_map/ppermute | solution.py:21
  39.0 2.8 gather_fusion.2
  41.8 2.6 copy.33
  44.5 151.0 %all-reduce.4.cloned.1.call-done = (bf16[2,128,1024]{2,1,0:T(8,128)(2,1)}, bf16[2,128,1024]{2,1,0:T(8,128)(2,1)}, bf16[2,128,1024]{2,1,0:T(8,128)(2,1)}, bf16[2,128,1024]{2,1,0:T(8,128)(2,1)}) async-done(((bf16[2,128,1024]{2,1,0:T(8,128)(2,1)}, bf16[2,128,1024]{2,1,0:T(8,128)(2,1)}, bf16[2,128,1024]{2,1,0:T(8,128)(2,1)}, bf16[2,128,1024]{2,1,0:T(8,128)(2,1)}), (bf16[2,128,1024]{2,1,0:T(8,128)(2,1)}, ...) | async-done | bytes 2097168 | tf_op jit(solution)/shard_map/psum | solution.py:28
  203.7 3.5 %pad_maximum_fusion = bf16[2,1024,1024]{2,1,0:T(8,128)(2,1)} fusion(bf16[2,256,1024]{2,1,0:T(8,128)(2,1)} %collective-permute-done.1, bf16[1,512,1024]{2,1,0:T(8,128)(2,1)S(1)} %bitcast.63, bf16[1,512,1024]{2,1,0:T(8,128)(2,1)S(1)} %bitcast.60, bf16[2,256,1024]{2,1,0:T(8,128)(2,1)} %collective-permute-done), kind=kLoop, calls=%fused_computation.26 | loop fusion | flops 16777216 | bytes 8388608 | tf_op jit(solution)/shard_map/concatenate | solution.py:22
  207.2 129.5 %while.10 = (s32[]{:T(128)}, bf16[4,128,1024]{2,1,0:T(8,128)(2,1)}, s32[4]{0:T(128)S(1)}, bf16[2,1024,1024]{2,1,0:T(8,128)(2,1)}, bf16[2,128,1024]{1,2,0:T(8,128...) while((s32[]{:T(128)}, bf16[4,128,1024]{2,1,0:T(8,128)(2,1)}, ...), condition=%wide.region_7.8_spmd, body=%wide.region_4.7_spmd.sunk | while | flops 916720896 | bytes 49296764 | solution.py:76
  208.4 3.5 %constant_dynamic-slice_fusion.4 = bf16[2,640,1024]{2,1,0:T(8,128)(2,1)} fusion(bf16[2,1024,1024]{2,1,0:T(8,128)(2,1)} %get-tuple-element.222, s32[]{:T(128)S(6)} %select_n.133), kind=kLoop, calls=%fused_computation.22.clone.1 | loop fusion | bytes 5242884 | tf_op jit(solution)/shard_map/while/body/eval_jaxpr/dynamic_slice | solution.py:55
  212.0 4.4 %copy.46 = bf16[2,640,1024]{1,2,0:T(8,128)(2,1)} copy(bf16[2,640,1024]{2,1,0:T(8,128)(2,1)} %constant_dynamic-slice_fusion.4) | data formatting | bytes 5242880 | tf_op jit(solution)/shard_map/while/body/eval_jaxpr/dynamic_slice | solution.py:55
  226.5 3.0 fusion.39
  229.5 2.6 exponential_reduce_fusion.2
  232.1 6.6 %fusion.40 = bf16[8,128,128]{2,1,0:T(8,128)(2,1)S(1)} fusion(bf16[1152,8,128]{0,2,1:T(8,128)(2,1)} %bitcast.57, f32[8,128]{1,0:T(8,128)S(1)} %exponential_reduce_fusion.2, f32[8,128,1152]{2,1,0:T(8,128)} %fusion.39), kind=kOutput, calls=%fused_computation.11.clone.1 | convolution fusion | flops 305662080 | bytes 7344128 | tf_op jit(solution)/shard_map/while/body/eval_jaxpr/hqk,khd->qhd/dot_general | solution.py:70
  240.8 3.5 %constant_dynamic-slice_fusion.4 = bf16[2,640,1024]{2,1,0:T(8,128)(2,1)} fusion(bf16[2,1024,1024]{2,1,0:T(8,128)(2,1)} %get-tuple-element.222, s32[]{:T(128)S(6)} %select_n.133), kind=kLoop, calls=%fused_computation.22.clone.1 | loop fusion | bytes 5242884 | tf_op jit(solution)/shard_map/while/body/eval_jaxpr/dynamic_slice | solution.py:55
  244.3 4.4 %copy.46 = bf16[2,640,1024]{1,2,0:T(8,128)(2,1)} copy(bf16[2,640,1024]{2,1,0:T(8,128)(2,1)} %constant_dynamic-slice_fusion.4) | data formatting | bytes 5242880 | tf_op jit(solution)/shard_map/while/body/eval_jaxpr/dynamic_slice | solution.py:55
  258.8 3.0 fusion.39
  261.9 2.6 exponential_reduce_fusion.2
  264.4 6.6 %fusion.40 = bf16[8,128,128]{2,1,0:T(8,128)(2,1)S(1)} fusion(bf16[1152,8,128]{0,2,1:T(8,128)(2,1)} %bitcast.57, f32[8,128]{1,0:T(8,128)S(1)} %exponential_reduce_fusion.2, f32[8,128,1152]{2,1,0:T(8,128)} %fusion.39), kind=kOutput, calls=%fused_computation.11.clone.1 | convolution fusion | flops 305662080 | bytes 7344128 | tf_op jit(solution)/shard_map/while/body/eval_jaxpr/hqk,khd->qhd/dot_general | solution.py:70
  273.2 3.5 %constant_dynamic-slice_fusion.4 = bf16[2,640,1024]{2,1,0:T(8,128)(2,1)} fusion(bf16[2,1024,1024]{2,1,0:T(8,128)(2,1)} %get-tuple-element.222, s32[]{:T(128)S(6)} %select_n.133), kind=kLoop, calls=%fused_computation.22.clone.1 | loop fusion | bytes 5242884 | tf_op jit(solution)/shard_map/while/body/eval_jaxpr/dynamic_slice | solution.py:55
  276.7 4.4 %copy.46 = bf16[2,640,1024]{1,2,0:T(8,128)(2,1)} copy(bf16[2,640,1024]{2,1,0:T(8,128)(2,1)} %constant_dynamic-slice_fusion.4) | data formatting | bytes 5242880 | tf_op jit(solution)/shard_map/while/body/eval_jaxpr/dynamic_slice | solution.py:55
  291.2 3.0 fusion.39
  294.2 2.6 exponential_reduce_fusion.2
  296.8 6.6 %fusion.40 = bf16[8,128,128]{2,1,0:T(8,128)(2,1)S(1)} fusion(bf16[1152,8,128]{0,2,1:T(8,128)(2,1)} %bitcast.57, f32[8,128]{1,0:T(8,128)S(1)} %exponential_reduce_fusion.2, f32[8,128,1152]{2,1,0:T(8,128)} %fusion.39), kind=kOutput, calls=%fused_computation.11.clone.1 | convolution fusion | flops 305662080 | bytes 7344128 | tf_op jit(solution)/shard_map/while/body/eval_jaxpr/hqk,khd->qhd/dot_general | solution.py:70
  305.5 3.5 %constant_dynamic-slice_fusion.4 = bf16[2,640,1024]{2,1,0:T(8,128)(2,1)} fusion(bf16[2,1024,1024]{2,1,0:T(8,128)(2,1)} %get-tuple-element.222, s32[]{:T(128)S(6)} %select_n.133), kind=kLoop, calls=%fused_computation.22.clone.1 | loop fusion | bytes 5242884 | tf_op jit(solution)/shard_map/while/body/eval_jaxpr/dynamic_slice | solution.py:55
  309.1 4.4 %copy.46 = bf16[2,640,1024]{1,2,0:T(8,128)(2,1)} copy(bf16[2,640,1024]{2,1,0:T(8,128)(2,1)} %constant_dynamic-slice_fusion.4) | data formatting | bytes 5242880 | tf_op jit(solution)/shard_map/while/body/eval_jaxpr/dynamic_slice | solution.py:55
  323.6 3.0 fusion.39
  326.6 2.6 exponential_reduce_fusion.2
  329.2 6.6 %fusion.40 = bf16[8,128,128]{2,1,0:T(8,128)(2,1)S(1)} fusion(bf16[1152,8,128]{0,2,1:T(8,128)(2,1)} %bitcast.57, f32[8,128]{1,0:T(8,128)S(1)} %exponential_reduce_fusion.2, f32[8,128,1152]{2,1,0:T(8,128)} %fusion.39), kind=kOutput, calls=%fused_computation.11.clone.1 | convolution fusion | flops 305662080 | bytes 7344128 | tf_op jit(solution)/shard_map/while/body/eval_jaxpr/hqk,khd->qhd/dot_general | solution.py:70
  336.7 4.2 %scatter_custom_fusion = bf16[512,1024]{1,0:T(8,128)(2,1)} fusion(s32[512]{0:T(512)S(1)} %compare_select_fusion, bf16[512,1024]{1,0:T(8,128)(2,1)} %bitcast.67, bf16[]{:T(256)} %constant.106.clone.1), kind=kCustom, calls=%fused_computation.49 | custom fusion | bytes 1049088 | tf_op jit(solution)/shard_map/scatter | solution.py:79
  (84 shorter events, 56.4 us)
Async XLA Ops:
  6.5 12.4 %copy-start = (bf16[512,1024]{1,0:T(8,128)(2,1)S(1)}, bf16[512,1024]{1,0:T(8,128)(2,1)}, u32[]{:S(2)}) copy-start(bf16[512,1024]{1,0:T(8,128)(2,1)} %param.8) | copy-start | bytes 3145732
  6.5 189.0 %all-reduce.4.cloned.1.call-start = ((), (), s32[]{:S(2)}) async-start(), calls=%async_computation | async-start | bytes 4194304 | tf_op jit(solution)/shard_map/psum | solution.py:28
  18.9 2.1 copy-start.1
  23.8 15.2 %copy-start.2 = (bf16[512,1024]{1,0:T(8,128)(2,1)S(1)}, bf16[512,1024]{1,0:T(8,128)(2,1)}, u32[]{:S(2)}) copy-start(bf16[512,1024]{1,0:T(8,128)(2,1)} %param.7) | copy-start | bytes 3145732
  29.7 174.0 %collective-permute-start = (bf16[2,256,1024]{2,1,0:T(8,128)(2,1)}, bf16[2,256,1024]{2,1,0:T(8,128)(2,1)}, u32[]{:S(2)}, u32[]{:S(2)}) collective-permute-start(bf16[2,256,1024]{2,1,0:T(8,128)(2,1)} %get-tuple-element.118), channel_id=1, source_target_pairs={{0,1},{1,2},{2,3},{3,4},{4,5},{5,6},{6,7},{7,8},{8,9},{9,10},{10,1... | collective-permute-start | bytes 3145736 | tf_op jit(solution)/shard_map/ppermute | solution.py:18
  33.2 170.5 %collective-permute-start.1 = (bf16[2,256,1024]{2,1,0:T(8,128)(2,1)}, bf16[2,256,1024]{2,1,0:T(8,128)(2,1)}, u32[]{:S(2)}, u32[]{:S(2)}) collective-permute-start(bf16[2,256,1024]{2,1,0:T(8,128)(2,1)} %get-tuple-element.119), channel_id=1, source_target_pairs={{1,0},{2,1},{3,2},{4,3},{5,4},{6,5},{7,6},{8,7},{9,8},{10,9},{11,1... | collective-permute-start | bytes 3145736 | tf_op jit(solution)/shard_map/ppermute | solution.py:21
  39.0 5.4 %copy-start.5 = (s32[4,9]{1,0:T(4,128)S(1)}, s32[4,9]{1,0:T(4,128)}, u32[]{:S(2)}) copy-start(s32[4,9]{1,0:T(4,128)} %param.10) | copy-start | bytes 436
  41.8 161.8 %copy-start.4 = (bf16[512,1024]{1,0:T(8,128)(2,1)S(1)}, bf16[512,1024]{1,0:T(8,128)(2,1)}, u32[]{:S(2)}) copy-start(bf16[512,1024]{1,0:T(8,128)(2,1)} %gather_fusion.1) | copy-start | bytes 3145732
  225.8 0.7 copy-start.3
  258.1 0.7 copy-start.3
  290.5 0.7 copy-start.3
  322.9 0.7 copy-start.3
Sparse Core Ops, SparseCore 0:
  27.1 168.3 all-reduce.3
where the time goes:
time: 351 us; the launch traced here: 348 us
  waiting for transfers between devices  151 us (43%)
  local copies, waits for them, and re-layouts  102 us (29%)
  matrix products  48.7 us (14%)
  between operations  23.6 us (7%)
  other arithmetic  10.1 us (3%)
  starting transfers between devices  9.33 us (3%)
    psum x1, waiting for transfers between devices, spread(): return lax.psum(jnp.where(mine, array, jnp.zeros_like(array)), axis)  151 us
    dynamic_slice x8, local copies, waits for them, and re-layouts, one_tile(): lax.dynamic_slice_in_dim(padded, tile_number * TILE_POINTS, (2 * BAND + 1...  31.9 us
    dot_general x4, matrix products, one_tile(): jnp.einsum('hqk,khd->qhd', weights, value_heads, preferred_element_type=j...  26.4 us
    while x24, local copies, waits for them, and re-layouts  24.3 us
    dot_general x4, matrix products, one_tile(): jnp.einsum('qhd,khd->hqk', queries_here, key_heads, preferred_element_typ...  12 us
    sub x4, matrix products, one_tile(): exponent = jnp.exp(scores - row_peak)  10.3 us
    while x4, local copies, waits for them, and re-layouts, body(): lax.map(one_tile, (tile_numbers, query_tiles, band_valid))  8.17 us
  transfers between devices with their start and end apart: 3, of which 1 were waited for; matrix products, arithmetic and copies ran while one was open for 5% of the time, Pallas kernels for 0%

commit v1 on v0

v1 whole, which is shorter than its diff:
```python
import functools

import jax
import jax.numpy as jnp
from jax import lax
from jax.experimental import pallas as pl
from jax.experimental.pallas import tpu as pltpu
from jax.sharding import PartitionSpec as P

LOCAL_HEADS = 8
HEAD_WIDTH = 128
TILE_POINTS = 128
BAND = 2
NG = 4
HALO = BAND * TILE_POINTS
PAIR = 2 * HEAD_WIDTH
MASKED = -1e30
EXP_SCALE = HEAD_WIDTH ** (-0.5) * 1.4426950408889634
VMEM_LIMIT = 48 * 1024 * 1024


def mm(a, b):
    return lax.dot_general(a, b, (((1,), (0,)), ((), ())), preferred_element_type=jnp.float32)


def mm_nt(a, b):
    return lax.dot_general(a, b, (((1,), (1,)), ((), ())), preferred_element_type=jnp.float32)


def pick_rows(order_ref):
    count = order_ref.shape[1]
    order = jnp.bitwise_and(order_ref[...], count - 1)
    column = jnp.transpose(jnp.broadcast_to(order, (128, count)))
    lane = lax.broadcasted_iota(jnp.int32, (count, 128), 1)
    parts = [column == lane + start for start in range(0, count, 128)]
    return jnp.concatenate([p.astype(jnp.float32) for p in parts], axis=1).astype(jnp.bfloat16)


def place_rows(order_ref):
    count = order_ref.shape[1]
    order = jnp.bitwise_and(order_ref[...], count - 1)
    row = lax.broadcasted_iota(jnp.int32, (count, count), 0)
    return (row == order).astype(jnp.float32).astype(jnp.bfloat16)


def bias_rows(lists_ref, query_tile, key_tiles):
    parts = []
    for key_tile in key_tiles:
        slot = key_tile - query_tile + BAND
        if 0 <= slot <= 2 * BAND:
            value = jnp.where(lists_ref[query_tile, slot] >= 0, 0.0, MASKED).astype(jnp.float32)
        else:
            value = jnp.float32(MASKED)
        parts.append(jnp.full((1, TILE_POINTS), value, jnp.float32))
    return jnp.concatenate(parts, axis=1)


def add_bias(scores, lists_ref, query_tiles, key_tiles):
    parts = []
    for at, query_tile in enumerate(query_tiles):
        rows = scores[at * TILE_POINTS : (at + 1) * TILE_POINTS]
        parts.append(rows + bias_rows(lists_ref, query_tile, key_tiles))
    return jnp.concatenate(parts, axis=0)


def sort_kernel(spot_ref, order_ref, k_ref, v_ref, head_ref, tail_ref, *rest):
    pieces, (pick, sorted_kv) = rest[:-2], rest[-2:]

    @pl.when(pl.program_id(0) == 0)
    def _():
        pick[...] = pick_rows(order_ref)

    count = k_ref.shape[0]
    for which, ref in enumerate((k_ref, v_ref)):
        rows = mm(pick[...], ref[...]).astype(jnp.bfloat16)
        sorted_kv[which] = rows
        head_ref[which] = rows[:HALO]
        tail_ref[which] = rows[count - HALO :]
    piece_rows = TILE_POINTS // len(pieces)
    for step, piece_ref in enumerate(pieces):
        number = lax.rem(spot_ref[1] + step, len(pieces))
        start = pl.multiple_of(spot_ref[0] * TILE_POINTS + number * piece_rows, piece_rows)
        piece_ref[...] = sorted_kv[:, pl.ds(start, piece_rows), :]


def local_kernel(lists_ref, order_ref, q_ref, head_ref, tail_ref, qs_ref, acc_ref, ml_ref, pick):
    step = pl.program_id(0)

    @pl.when(step == 0)
    def _():
        pick[...] = pick_rows(order_ref)
        ml_ref[...] = jnp.zeros_like(ml_ref)

    queries = mm(pick[...], q_ref[...]).astype(jnp.bfloat16)
    qs_ref[...] = queries
    tiles = range(q_ref.shape[0] // TILE_POINTS)
    lane = lax.broadcasted_iota(jnp.int32, ml_ref.shape, 1)
    for at in range(PAIR // HEAD_WIDTH):
        cols = slice(at * HEAD_WIDTH, (at + 1) * HEAD_WIDTH)
        keys = jnp.concatenate([head_ref[0, :, cols], tail_ref[0, :, cols]], axis=0)
        values = jnp.concatenate([head_ref[1, :, cols], tail_ref[1, :, cols]], axis=0)
        scores = add_bias(mm_nt(queries[:, cols], keys), lists_ref, tiles, tiles)
        peak = jnp.max(scores, axis=1, keepdims=True)
        weights = jnp.exp2((scores - peak) * EXP_SCALE)
        total = jnp.sum(weights, axis=1, keepdims=True)
        acc_ref[:, cols] = mm(weights.astype(jnp.bfloat16), values)
        head = step * (PAIR // HEAD_WIDTH) + at
        kept = jnp.where(lane == head, peak, ml_ref[...])
        ml_ref[...] = jnp.where(lane == head + LOCAL_HEADS, total, kept)


def finish_kernel(lists_ref, order_ref, qs_ref, acc_ref, ml_ref, low_ref, high_ref, *rest):
    pieces, (out_ref, place) = rest[:-2], rest[-2:]
    step = pl.program_id(0)

    @pl.when(step == 0)
    def _():
        place[...] = place_rows(order_ref)

    count = qs_ref.shape[0]
    tiles_here = count // TILE_POINTS
    lane = lax.broadcasted_iota(jnp.int32, ml_ref.shape, 1)
    results = []
    for at in range(PAIR // HEAD_WIDTH):
        cols = slice(at * HEAD_WIDTH, (at + 1) * HEAD_WIDTH)
        head = step * (PAIR // HEAD_WIDTH) + at
        ml = ml_ref[...]
        old_peak = jnp.sum(jnp.where(lane == head, ml, 0.0), axis=1, keepdims=True)
        old_total = jnp.sum(jnp.where(lane == head + LOCAL_HEADS, ml, 0.0), axis=1, keepdims=True)
        queries = qs_ref[:, cols]
        global_keys = jnp.concatenate([ref[0, :, cols] for ref in pieces], axis=0)
        global_values = jnp.concatenate([ref[1, :, cols] for ref in pieces], axis=0)
        far = mm_nt(queries, global_keys)
        low = add_bias(
            mm_nt(queries[:HALO], low_ref[0, :, cols]), lists_ref, range(BAND), range(-BAND, 0)
        )
        high = add_bias(
            mm_nt(queries[count - HALO :], high_ref[0, :, cols]),
            lists_ref,
            range(tiles_here - BAND, tiles_here),
            range(tiles_here, tiles_here + BAND),
        )
        near_peak = jnp.concatenate(
            [jnp.max(low, axis=1, keepdims=True), jnp.max(high, axis=1, keepdims=True)], axis=0
        )
        peak = jnp.maximum(jnp.maximum(old_peak, near_peak), jnp.max(far, axis=1, keepdims=True))
        shrink = jnp.exp2((old_peak - peak) * EXP_SCALE)
        far = jnp.exp2((far - peak) * EXP_SCALE)
        low = jnp.exp2((low - peak[:HALO]) * EXP_SCALE)
        high = jnp.exp2((high - peak[count - HALO :]) * EXP_SCALE)
        near_total = jnp.concatenate(
            [jnp.sum(low, axis=1, keepdims=True), jnp.sum(high, axis=1, keepdims=True)], axis=0
        )
        total = old_total * shrink + near_total + jnp.sum(far, axis=1, keepdims=True)
        near_sum = jnp.concatenate(
            [
                mm(low.astype(jnp.bfloat16), low_ref[1, :, cols]),
                mm(high.astype(jnp.bfloat16), high_ref[1, :, cols]),
            ],
            axis=0,
        )
        summed = acc_ref[:, cols] * shrink + near_sum + mm(far.astype(jnp.bfloat16), global_values)
        results.append((summed / total).astype(jnp.bfloat16))
    attended = jnp.concatenate(results, axis=1)
    out_ref[...] = mm(place[...], attended).astype(jnp.bfloat16)


def column_block(*leading):
    zeros = (0,) * len(leading)
    return pl.BlockSpec((*leading, PAIR), lambda i: (*zeros, i))


def whole_block(*shape):
    return pl.BlockSpec(shape, lambda i: (0,) * len(shape))


SCALARS = pl.BlockSpec(memory_space=pltpu.SMEM)


def spread_along(piece, axis, root):
    count = lax.axis_size(axis)
    at = lax.axis_index(axis)
    middle = count // 2
    for i in range(middle - 1):
        got = lax.ppermute(piece, axis, [(i, i + 1), (count - 1 - i, count - 2 - i)])
        take = ((at == i + 1) & (root <= i)) | ((at == count - 2 - i) & (root >= count - 1 - i))
        piece = jnp.where(take, got, piece)
    got = lax.ppermute(piece, axis, [(middle - 1, middle), (middle, middle - 1)])
    take = ((at == middle) & (root < middle)) | ((at == middle - 1) & (root >= middle))
    piece = jnp.where(take, got, piece)
    for i in range(middle - 1, 0, -1):
        got = lax.ppermute(piece, axis, [(i, i - 1), (count - 1 - i, count - i)])
        take = ((at == i - 1) & (root >= i)) | ((at == count - i) & (root <= count - 1 - i))
        piece = jnp.where(take, got, piece)
    return piece


def body(query_rows, key_rows, value_rows, tile_lists, hilbert_order):
    row_count, feature_count = query_rows.shape
    tiles_here = row_count // TILE_POINTS
    blk_count, grp_count = lax.axis_size("blk"), lax.axis_size("grp")
    part = blk_count // NG
    steps = feature_count // PAIR
    grid = (steps,)
    params = pltpu.CompilerParams(vmem_limit_bytes=VMEM_LIMIT)
    bf16 = functools.partial(jax.ShapeDtypeStruct, dtype=jnp.bfloat16)
    f32 = functools.partial(jax.ShapeDtypeStruct, dtype=jnp.float32)

    order = hilbert_order.reshape(1, row_count)
    tile_id = tile_lists[0, 2 * BAND + 1] % (tiles_here * blk_count * grp_count // NG)
    owner, owner_tile = tile_id // tiles_here, tile_id % tiles_here
    owner_blk, owner_grp = owner // grp_count, owner % grp_count
    my_part = lax.axis_index("blk") % part
    spot = jnp.stack([owner_tile, my_part]).astype(jnp.int32)

    piece_rows = TILE_POINTS // part
    head, tail, *pieces = pl.pallas_call(
        sort_kernel,
        grid=grid,
        in_specs=[
            SCALARS,
            whole_block(1, row_count),
            column_block(row_count),
            column_block(row_count),
        ],
        out_specs=[column_block(2, HALO)] * 2 + [column_block(2, piece_rows)] * part,
        out_shape=[bf16((2, HALO, feature_count))] * 2
        + [bf16((2, piece_rows, feature_count))] * part,
        scratch_shapes=[
            pltpu.VMEM((row_count, row_count), jnp.bfloat16),
            pltpu.VMEM((2, row_count, PAIR), jnp.bfloat16),
        ],
        compiler_params=params,
        name="sort_keys_values",
    )(spot, order, key_rows, value_rows)

    piece = pieces[0]
    for step in range(1, part):
        pairs = [(i, i // part * part + (i + step) % part) for i in range(blk_count)]
        got = lax.ppermute(pieces[step], "blk", pairs)
        piece = jnp.where((my_part - step) % part == owner_blk, got, piece)
    piece = spread_along(piece, "grp", owner_grp)

    axes = ("blk", "grp")
    count = blk_count * grp_count
    forward = [(i, i + 1) for i in range(count - 1)]
    low = lax.ppermute(tail, axes, forward)
    high = lax.ppermute(head, axes, [(target, source) for source, target in forward])

    gathered = [piece]
    for quarter in range(1, NG):
        pairs = [(i, (i // part ^ quarter) * part + i % part) for i in range(blk_count)]
        gathered.append(lax.ppermute(piece, "blk", pairs))
    quarters = jnp.concatenate(gathered, axis=1)
    global_pieces = [quarters]
    for step in range(1, part):
        pairs = [(i, i // part * part + (i + step) % part) for i in range(blk_count)]
        global_pieces.append(lax.ppermute(quarters, "blk", pairs))

    queries, summed, peaks = pl.pallas_call(
        local_kernel,
        grid=grid,
        in_specs=[
            SCALARS,
            whole_block(1, row_count),
            column_block(row_count),
            column_block(2, HALO),
            column_block(2, HALO),
        ],
        out_specs=[column_block(row_count), column_block(row_count), whole_block(row_count, 128)],
        out_shape=[
            bf16((row_count, feature_count)),
            f32((row_count, feature_count)),
            f32((row_count, 128)),
        ],
        scratch_shapes=[pltpu.VMEM((row_count, row_count), jnp.bfloat16)],
        compiler_params=params,
        name="attend_own",
    )(tile_lists, order, query_rows, head, tail)

    return pl.pallas_call(
        finish_kernel,
        grid=grid,
        in_specs=[
            SCALARS,
            whole_block(1, row_count),
            column_block(row_count),
            column_block(row_count),
            whole_block(row_count, 128),
            column_block(2, HALO),
            column_block(2, HALO),
        ]
        + [column_block(2, NG * piece_rows)] * part,
        out_specs=column_block(row_count),
        out_shape=bf16((row_count, feature_count)),
        scratch_shapes=[pltpu.VMEM((row_count, row_count), jnp.bfloat16)],
        compiler_params=params,
        name="attend_rest",
    )(tile_lists, order, queries, summed, peaks, low, high, *global_pieces)


def solution(mesh):
    rows = P(("blk", "grp"), None)
    in_specs = (rows, rows, rows, rows, P(("blk", "grp")))
    return jax.shard_map(body, mesh=mesh, in_specs=in_specs, out_specs=rows, check_vma=False)
```

time: 351 us -> 108 us (0.31)
  local copies, waits for them, and re-layouts: 102 us -> 4.4 us
  waiting for transfers between devices: 151 us -> 54.4 us
  matrix products: 48.7 us -> 0 us
  Pallas kernels: 0 us -> 22.8 us
  between operations: 23.6 us -> 2.18 us
  starting transfers between devices: 9.33 us -> 19.7 us
  other arithmetic: 10.1 us -> 2.89 us
    psum x1 -> x0, waiting for transfers between devices: 151 us -> none  [spread(): return lax.psum(jnp.where(mine, array, jnp.zeros_like(array)), axis)]
    ppermute x2 -> x10, waiting for transfers between devices: 0.01 us -> 54.4 us  [the longest x1 17.2 us: body(): lax.ppermute(head, axes, [(target, source) for source, target in forward])]
    dot_general x8 -> x0, matrix products: 38.4 us -> none  [the longest x4 26.4 us: one_tile(): jnp.einsum('hqk,khd->qhd', weights, value_heads, preferred_element_type=j...]
    dynamic_slice x16 -> x0, local copies, waits for them, and re-layouts: 38.1 us -> none  [the longest x8 31.9 us: one_tile(): lax.dynamic_slice_in_dim(padded, tile_number * TILE_POINTS, (2 * BAND + 1...]
    while x28 -> x0, local copies, waits for them, and re-layouts: 32.4 us -> none
    pallas_call x0 -> x3, Pallas kernels: none -> 22.8 us  [the longest x1 12.7 us: body(): pl.pallas_call(finish_kernel, grid=grid, in_specs=[SCALARS, whole_block(1...]
    ppermute x2 -> x10, starting transfers between devices: 9.33 us -> 19.7 us  [the longest x1 7.24 us: body(): lax.ppermute(head, axes, [(target, source) for source, target in forward])]
    sub x4 -> x0, matrix products: 10.3 us -> none  [one_tile(): exponent = jnp.exp(scores - row_peak)]
  transfers between devices with their start and end apart: 3 -> 10, of which waited for: 1 -> 6; matrix products, arithmetic and copies ran while one was open for 5% -> 0% of each run, Pallas kernels for 0% -> 7%
where the time goes in v1:
time: 108 us; the launch traced here: 106 us
  waiting for transfers between devices  54.4 us (50%)
  Pallas kernels  22.8 us (21%)
  starting transfers between devices  19.7 us (18%)
  local copies, waits for them, and re-layouts  4.4 us (4%)
  other arithmetic  2.89 us (3%)
  between operations  2.18 us (2%)
    ppermute x1, waiting for transfers between devices, body(): lax.ppermute(head, axes, [(target, source) for source, target in forward])  17.2 us
    ppermute x1, waiting for transfers between devices, spread_along(): got = lax.ppermute(piece, axis, [(i, i - 1), (count - 1 - i, count - i)])  15.9 us
    ppermute x1, waiting for transfers between devices, body(): low = lax.ppermute(tail, axes, forward)  14.5 us
    pallas_call x1, Pallas kernels, body(): pl.pallas_call(finish_kernel, grid=grid, in_specs=[SCALARS, whole_block(1...  12.7 us
    ppermute x1, starting transfers between devices, body(): lax.ppermute(head, axes, [(target, source) for source, target in forward])  7.24 us
    pallas_call x1, Pallas kernels, body(): pl.pallas_call(local_kernel, grid=grid, in_specs=[SCALARS, whole_block(1,...  6.97 us
    ppermute x1, waiting for transfers between devices, spread_along(): lax.ppermute(piece, axis, [(i, i + 1), (count - 1 - i, count - 2 - i)])  5.15 us
    ppermute x1, starting transfers between devices, spread_along(): lax.ppermute(piece, axis, [(i, i + 1), (count - 1 - i, count - 2 - i)])  4.18 us
  transfers between devices with their start and end apart: 10, of which 6 were waited for; matrix products, arithmetic and copies ran while one was open for 0% of the time, Pallas kernels for 7%

profile of v1, /device:TPU:4, one launch (start us, length us, event | category | flops | bytes accessed | tf_op | source)
XLA Modules:
  0.0 106.4 jit_solution(5187377389930637627)
XLA Ops:
  0.0 1.3 %slice.3 = s32[1,1]{1,0:T(1,128)} slice(s32[4,9]{1,0:T(4,128)} %lists_ref.3), slice={[0:1], [5:6]} | slice | bytes 8 | tf_op jit(solution)/shard_map/slice | solution.py:210
  3.2 0.1 pad_add_fusion.spot_ref
  3.3 1.2 %copy-done = bf16[512,1024]{1,0:T(8,128)(2,1)S(1)} copy-done((bf16[512,1024]{1,0:T(8,128)(2,1)S(1)}, bf16[512,1024]{1,0:T(8,128)(2,1)}, u32[]{:S(2)}) %copy-start) | copy-done | bytes 1048600
  4.6 1.2 %copy-done.1 = bf16[512,1024]{1,0:T(8,128)(2,1)S(1)} copy-done((bf16[512,1024]{1,0:T(8,128)(2,1)S(1)}, bf16[512,1024]{1,0:T(8,128)(2,1)}, u32[]{:S(2)}) %copy-start.1) | copy-done | bytes 1048600
  5.8 0.7 copy-done.3
  6.5 3.1 %sort_keys_values.1 = (bf16[2,256,1024]{2,1,0:T(8,128)(2,1)S(1)}, bf16[2,256,1024]{2,1,0:T(8,128)(2,1)S(1)}, bf16[2,64,1024]{2,1,0:T(8,128)(2,1)S(1)}, bf16[2,64,1024]{2,1,0:T(8,128)(2,1)S(1)}) custom-call(s32[2]{0:T(128)S(1)} %pad_add_fusion.spot_ref, s32[1,512]{1,0:T(1,128)S(1)} %bitcast.4, bf16[512,1024]{1,0:T(8,128)(2,1)S(1)} %copy-done, ...), custom_call_target="tpu_custom_call" | custom-call | tf_op jit(solution)/shard_map/sort_keys_values/pallas_call | solution.py:217
  9.6 0.1 collective-permute-start.2
  9.7 1.5 %collective-permute-done.2 = bf16[2,64,1024]{2,1,0:T(8,128)(2,1)S(1)} collective-permute-done((bf16[2,64,1024]{2,1,0:T(8,128)(2,1)S(1)}, bf16[2,64,1024]{2,1,0:T(8,128)(2,1)S(1)}, u32[]{:S(2)}, u32[]{:S(2)}) %collective-permute-start.2) | collective-permute-done | bytes 262176 | tf_op jit(solution)/shard_map/ppermute | solution.py:240
  11.2 4.2 %collective-permute-start.3 = (bf16[2,64,1024]{2,1,0:T(8,128)(2,1)S(1)}, bf16[2,64,1024]{2,1,0:T(8,128)(2,1)}, u32[]{:S(2)}, u32[]{:S(2)}) collective-permute-start(bf16[2,64,1024]{2,1,0:T(8,128)(2,1)S(1)} %broadcast_select_fusion), channel_id=1, source_target_pairs={{0,1},{3,2},{4,5},{7,6},{8,9},{11,10},{12,13},{15,14},{16,17},{19,... | collective-permute-start | bytes 786440 | tf_op jit(solution)/shard_map/ppermute | solution.py:185
  15.4 5.2 %collective-permute-done.3 = bf16[2,64,1024]{2,1,0:T(8,128)(2,1)} collective-permute-done((bf16[2,64,1024]{2,1,0:T(8,128)(2,1)S(1)}, bf16[2,64,1024]{2,1,0:T(8,128)(2,1)}, u32[]{:S(2)}, u32[]{:S(2)}) %collective-permute-start.3) | collective-permute-done | bytes 262176 | tf_op jit(solution)/shard_map/ppermute | solution.py:185
  20.6 0.7 broadcast_select_fusion.1
  21.3 1.3 %collective-permute-start.4 = (bf16[2,64,1024]{2,1,0:T(8,128)(2,1)}, bf16[2,64,1024]{2,1,0:T(8,128)(2,1)}, u32[]{:S(2)}, u32[]{:S(2)}) collective-permute-start(bf16[2,64,1024]{2,1,0:T(8,128)(2,1)} %broadcast_select_fusion.1), channel_id=1, source_target_pairs={{1,2},{2,1},{5,6},{6,5},{9,10},{10,9},{13,14},{14,13},{17,18},{18,... | collective-permute-start | bytes 786440 | tf_op jit(solution)/shard_map/ppermute | solution.py:188
  22.6 0.0 collective-permute-done.4
  22.7 1.0 broadcast_select_fusion.2
  23.6 1.3 %collective-permute-start.5 = (bf16[2,64,1024]{2,1,0:T(8,128)(2,1)S(1)}, bf16[2,64,1024]{2,1,0:T(8,128)(2,1)}, u32[]{:S(2)}, u32[]{:S(2)}) collective-permute-start(bf16[2,64,1024]{2,1,0:T(8,128)(2,1)S(1)} %broadcast_select_fusion.2), channel_id=1, source_target_pairs={{1,0},{2,3},{5,4},{6,7},{9,8},{10,11},{13,12},{14,15},{17,16},{18,... | collective-permute-start | bytes 786440 | tf_op jit(solution)/shard_map/ppermute | solution.py:192
  25.0 15.9 %collective-permute-done.5 = bf16[2,64,1024]{2,1,0:T(8,128)(2,1)} collective-permute-done((bf16[2,64,1024]{2,1,0:T(8,128)(2,1)S(1)}, bf16[2,64,1024]{2,1,0:T(8,128)(2,1)}, u32[]{:S(2)}, u32[]{:S(2)}) %collective-permute-start.5) | collective-permute-done | bytes 262176 | tf_op jit(solution)/shard_map/ppermute | solution.py:192
  40.8 1.0 broadcast_select_fusion.3
  41.8 1.5 %collective-permute-start.8 = (bf16[2,64,1024]{2,1,0:T(8,128)(2,1)S(1)}, bf16[2,64,1024]{2,1,0:T(8,128)(2,1)S(1)}, u32[]{:S(2)}, u32[]{:S(2)}) collective-permute-start(bf16[2,64,1024]{2,1,0:T(8,128)(2,1)S(1)} %broadcast_select_fusion.3), channel_id=1, source_target_pairs={{0,24},{4,28},{8,16},{12,20},{16,8},{20,12},{24,0},{28,4},{1,25},{... | collective-permute-start | bytes 786440 | tf_op jit(solution)/shard_map/ppermute | solution.py:253
  43.3 1.5 %collective-permute-start.7 = (bf16[2,64,1024]{2,1,0:T(8,128)(2,1)S(1)}, bf16[2,64,1024]{2,1,0:T(8,128)(2,1)S(1)}, u32[]{:S(2)}, u32[]{:S(2)}) collective-permute-start(bf16[2,64,1024]{2,1,0:T(8,128)(2,1)S(1)} %broadcast_select_fusion.3), channel_id=1, source_target_pairs={{0,16},{4,20},{8,24},{12,28},{16,0},{20,4},{24,8},{28,12},{1,17},{... | collective-permute-start | bytes 786440 | tf_op jit(solution)/shard_map/ppermute | solution.py:253
  44.8 0.5 collective-permute-start.6
  45.4 1.9 %collective-permute-start = (bf16[2,256,1024]{2,1,0:T(8,128)(2,1)S(1)}, bf16[2,256,1024]{2,1,0:T(8,128)(2,1)S(1)}, u32[]{:S(2)}, u32[]{:S(2)}) collective-permute-start(bf16[2,256,1024]{2,1,0:T(8,128)(2,1)S(1)} %get-tuple-element.13.tail_ref), channel_id=1, source_target_pairs={{0,1},{1,2},{2,3},{3,4},{4,5},{5,6},{6,7},{7,8},{8,9},{9,10},{10,1... | collective-permute-start | bytes 3145736 | tf_op jit(solution)/shard_map/ppermute | solution.py:247
  47.3 7.2 %collective-permute-start.1 = (bf16[2,256,1024]{2,1,0:T(8,128)(2,1)S(1)}, bf16[2,256,1024]{2,1,0:T(8,128)(2,1)S(1)}, u32[]{:S(2)}, u32[]{:S(2)}) collective-permute-start(bf16[2,256,1024]{2,1,0:T(8,128)(2,1)S(1)} %get-tuple-element.12.head_ref), channel_id=1, source_target_pairs={{1,0},{2,1},{3,2},{4,3},{5,4},{6,5},{7,6},{8,7},{9,8},{10,9},{11,1... | collective-permute-start | bytes 3145736 | tf_op jit(solution)/shard_map/ppermute | solution.py:248
  54.5 0.0 collective-permute-done.8
  54.5 0.2 collective-permute-done.7
  54.7 0.0 collective-permute-done.6
  54.7 0.1 pad_maximum_fusion.rest_0_
  54.8 0.1 collective-permute-start.9
  54.9 7.0 %attend_own.1 = (bf16[512,1024]{1,0:T(8,128)(2,1)S(1)}, f32[512,1024]{1,0:T(8,128)}, f32[512,128]{1,0:T(8,128)S(1)}) custom-call(s32[4,9]{1,0:T(4,128)S(1)} %copy-done.5, s32[1,512]{1,0:T(1,128)S(1)} %bitcast.5, bf16[512,1024]{1,0:T(8,128)(2,1)S(1)} %copy-done.2, bf16[2,256,1024]{2,1,0:T(8,128)(2,1)S(1)} %get-tuple-element.12.head_ref, ...), custom_call_target="tpu_custom_call" | custom-call | tf_op jit(solution)/shard_map/attend_own/pallas_call | solution.py:260
  61.9 14.5 %collective-permute-done.low_ref = bf16[2,256,1024]{2,1,0:T(8,128)(2,1)S(1)} collective-permute-done((bf16[2,256,1024]{2,1,0:T(8,128)(2,1)S(1)}, bf16[2,256,1024]{2,1,0:T(8,128)(2,1)S(1)}, u32[]{:S(2)}, u32[]{:S(2)}) %collective-permute-start) | collective-permute-done | bytes 1048608 | tf_op jit(solution)/shard_map/ppermute | solution.py:247
  76.4 17.2 %collective-permute-done.1.high_ref = bf16[2,256,1024]{2,1,0:T(8,128)(2,1)S(1)} collective-permute-done((bf16[2,256,1024]{2,1,0:T(8,128)(2,1)S(1)}, bf16[2,256,1024]{2,1,0:T(8,128)(2,1)S(1)}, u32[]{:S(2)}, u32[]{:S(2)}) %collective-permute-start.1) | collective-permute-done | bytes 1048608 | tf_op jit(solution)/shard_map/ppermute | solution.py:248
  93.6 0.0 collective-permute-done.9.rest_1_
  93.6 12.7 %attend_rest.1 = bf16[512,1024]{1,0:T(8,128)(2,1)} custom-call(s32[4,9]{1,0:T(4,128)S(1)} %copy-done.5, s32[1,512]{1,0:T(1,128)S(1)} %bitcast.6, bf16[512,1024]{1,0:T(8,128)(2,1)S(1)} %get-tuple-element.14.qs_ref, f32[512,1024]{1,0:T(8,128)} %get-tuple-element.15.acc_ref, f32[512,128]{1,0:T(8,128)S(1)} %get-tuple-element.16.ml_ref, ...), custom_call_target="tpu_custom_call" | custom-call | tf_op jit(solution)/shard_map/attend_rest/pallas_call | solution.py:281
  (10 shorter events, 0.0 us)
Async XLA Ops:
  3.3 1.2 %copy-start = (bf16[512,1024]{1,0:T(8,128)(2,1)S(1)}, bf16[512,1024]{1,0:T(8,128)(2,1)}, u32[]{:S(2)}) copy-start(bf16[512,1024]{1,0:T(8,128)(2,1)} %k_ref.1) | copy-start | bytes 3145732
  4.5 1.2 %copy-start.1 = (bf16[512,1024]{1,0:T(8,128)(2,1)S(1)}, bf16[512,1024]{1,0:T(8,128)(2,1)}, u32[]{:S(2)}) copy-start(bf16[512,1024]{1,0:T(8,128)(2,1)} %v_ref.1) | copy-start | bytes 3145732
  5.8 0.7 copy-start.3
  9.6 1.6 %collective-permute-start.2 = (bf16[2,64,1024]{2,1,0:T(8,128)(2,1)S(1)}, bf16[2,64,1024]{2,1,0:T(8,128)(2,1)S(1)}, u32[]{:S(2)}, u32[]{:S(2)}) collective-permute-start(bf16[2,64,1024]{2,1,0:T(8,128)(2,1)S(1)} %get-tuple-element.17), channel_id=1, source_target_pairs={{0,4},{4,0},{8,12},{12,8},{16,20},{20,16},{24,28},{28,24},{1,5},{5... | collective-permute-start | bytes 786440 | tf_op jit(solution)/shard_map/ppermute | solution.py:240
  11.2 9.3 %collective-permute-start.3 = (bf16[2,64,1024]{2,1,0:T(8,128)(2,1)S(1)}, bf16[2,64,1024]{2,1,0:T(8,128)(2,1)}, u32[]{:S(2)}, u32[]{:S(2)}) collective-permute-start(bf16[2,64,1024]{2,1,0:T(8,128)(2,1)S(1)} %broadcast_select_fusion), channel_id=1, source_target_pairs={{0,1},{3,2},{4,5},{7,6},{8,9},{11,10},{12,13},{15,14},{16,17},{19,... | collective-permute-start | bytes 786440 | tf_op jit(solution)/shard_map/ppermute | solution.py:185
  15.4 39.5 %copy-start.2 = (bf16[512,1024]{1,0:T(8,128)(2,1)S(1)}, bf16[512,1024]{1,0:T(8,128)(2,1)}, u32[]{:S(2)}) copy-start(bf16[512,1024]{1,0:T(8,128)(2,1)} %q_ref.1) | copy-start | bytes 3145732
  15.4 39.5 %copy-start.4 = (s32[512]{0:T(512)S(1)}, s32[512]{0:T(512)}, u32[]{:S(2)}) copy-start(s32[512]{0:T(512)} %param.9) | copy-start | bytes 6148
  15.4 39.5 %copy-start.5 = (s32[4,9]{1,0:T(4,128)S(1)}, s32[4,9]{1,0:T(4,128)}, u32[]{:S(2)}) copy-start(s32[4,9]{1,0:T(4,128)} %lists_ref.3) | copy-start | bytes 436
  21.3 1.4 %collective-permute-start.4 = (bf16[2,64,1024]{2,1,0:T(8,128)(2,1)}, bf16[2,64,1024]{2,1,0:T(8,128)(2,1)}, u32[]{:S(2)}, u32[]{:S(2)}) collective-permute-start(bf16[2,64,1024]{2,1,0:T(8,128)(2,1)} %broadcast_select_fusion.1), channel_id=1, source_target_pairs={{1,2},{2,1},{5,6},{6,5},{9,10},{10,9},{13,14},{14,13},{17,18},{18,... | collective-permute-start | bytes 786440 | tf_op jit(solution)/shard_map/ppermute | solution.py:188
  23.6 17.2 %collective-permute-start.5 = (bf16[2,64,1024]{2,1,0:T(8,128)(2,1)S(1)}, bf16[2,64,1024]{2,1,0:T(8,128)(2,1)}, u32[]{:S(2)}, u32[]{:S(2)}) collective-permute-start(bf16[2,64,1024]{2,1,0:T(8,128)(2,1)S(1)} %broadcast_select_fusion.2), channel_id=1, source_target_pairs={{1,0},{2,3},{5,4},{6,7},{9,8},{10,11},{13,12},{14,15},{17,16},{18,... | collective-permute-start | bytes 786440 | tf_op jit(solution)/shard_map/ppermute | solution.py:192
  41.8 12.7 %collective-permute-start.8 = (bf16[2,64,1024]{2,1,0:T(8,128)(2,1)S(1)}, bf16[2,64,1024]{2,1,0:T(8,128)(2,1)S(1)}, u32[]{:S(2)}, u32[]{:S(2)}) collective-permute-start(bf16[2,64,1024]{2,1,0:T(8,128)(2,1)S(1)} %broadcast_select_fusion.3), channel_id=1, source_target_pairs={{0,24},{4,28},{8,16},{12,20},{16,8},{20,12},{24,0},{28,4},{1,25},{... | collective-permute-start | bytes 786440 | tf_op jit(solution)/shard_map/ppermute | solution.py:253
  43.3 11.4 %collective-permute-start.7 = (bf16[2,64,1024]{2,1,0:T(8,128)(2,1)S(1)}, bf16[2,64,1024]{2,1,0:T(8,128)(2,1)S(1)}, u32[]{:S(2)}, u32[]{:S(2)}) collective-permute-start(bf16[2,64,1024]{2,1,0:T(8,128)(2,1)S(1)} %broadcast_select_fusion.3), channel_id=1, source_target_pairs={{0,16},{4,20},{8,24},{12,28},{16,0},{20,4},{24,8},{28,12},{1,17},{... | collective-permute-start | bytes 786440 | tf_op jit(solution)/shard_map/ppermute | solution.py:253
  44.8 9.9 %collective-permute-start.6 = (bf16[2,64,1024]{2,1,0:T(8,128)(2,1)S(1)}, bf16[2,64,1024]{2,1,0:T(8,128)(2,1)S(1)}, u32[]{:S(2)}, u32[]{:S(2)}) collective-permute-start(bf16[2,64,1024]{2,1,0:T(8,128)(2,1)S(1)} %broadcast_select_fusion.3), channel_id=1, source_target_pairs={{0,8},{4,12},{8,0},{12,4},{16,24},{20,28},{24,16},{28,20},{1,9},{5... | collective-permute-start | bytes 786440 | tf_op jit(solution)/shard_map/ppermute | solution.py:253
  45.4 31.0 %collective-permute-start = (bf16[2,256,1024]{2,1,0:T(8,128)(2,1)S(1)}, bf16[2,256,1024]{2,1,0:T(8,128)(2,1)S(1)}, u32[]{:S(2)}, u32[]{:S(2)}) collective-permute-start(bf16[2,256,1024]{2,1,0:T(8,128)(2,1)S(1)} %get-tuple-element.13.tail_ref), channel_id=1, source_target_pairs={{0,1},{1,2},{2,3},{3,4},{4,5},{5,6},{6,7},{7,8},{8,9},{9,10},{10,1... | collective-permute-start | bytes 3145736 | tf_op jit(solution)/shard_map/ppermute | solution.py:247
  47.3 46.3 %collective-permute-start.1 = (bf16[2,256,1024]{2,1,0:T(8,128)(2,1)S(1)}, bf16[2,256,1024]{2,1,0:T(8,128)(2,1)S(1)}, u32[]{:S(2)}, u32[]{:S(2)}) collective-permute-start(bf16[2,256,1024]{2,1,0:T(8,128)(2,1)S(1)} %get-tuple-element.12.head_ref), channel_id=1, source_target_pairs={{1,0},{2,1},{3,2},{4,3},{5,4},{6,5},{7,6},{8,7},{9,8},{10,9},{11,1... | collective-permute-start | bytes 3145736 | tf_op jit(solution)/shard_map/ppermute | solution.py:248
  54.8 38.9 %collective-permute-start.9 = (bf16[2,256,1024]{2,1,0:T(8,128)(2,1)S(1)}, bf16[2,256,1024]{2,1,0:T(8,128)(2,1)S(1)}, u32[]{:S(2)}, u32[]{:S(2)}) collective-permute-start(bf16[2,256,1024]{2,1,0:T(8,128)(2,1)S(1)} %pad_maximum_fusion.rest_0_), channel_id=1, source_target_pairs={{0,4},{4,0},{8,12},{12,8},{16,20},{20,16},{24,28},{28,24},{1,5},{5... | collective-permute-start | bytes 3145736 | tf_op jit(solution)/shard_map/ppermute | solution.py:258

commit v2 on v0

v2 whole, which is shorter than its diff:
```python
import functools

import jax
import jax.numpy as jnp
from jax import lax
from jax.experimental import pallas as pl
from jax.experimental.pallas import tpu as pltpu
from jax.sharding import PartitionSpec as P

LOCAL_HEADS = 8
HEAD_WIDTH = 128
TILE_POINTS = 128
BAND = 2
NG = 4
HALO = BAND * TILE_POINTS
PAIR_HEADS = 4
PAIR = PAIR_HEADS * HEAD_WIDTH
STATE_ROWS = 8
MASKED = -1e30
EXP_SCALE = HEAD_WIDTH ** (-0.5) * 1.4426950408889634
VMEM_LIMIT = 16 * 1024 * 1024


def mm(a, b):
    return lax.dot_general(a, b, (((1,), (0,)), ((), ())), preferred_element_type=jnp.float32)


def mm_tn(a, b):
    return lax.dot_general(a, b, (((0,), (0,)), ((), ())), preferred_element_type=jnp.float32)


def mm_nt(a, b):
    return lax.dot_general(a, b, (((1,), (1,)), ((), ())), preferred_element_type=jnp.float32)


def pick_rows(order):
    count = order.shape[1]
    column = jnp.transpose(jnp.broadcast_to(order, (128, count)))
    lane = lax.broadcasted_iota(jnp.int32, (count, 128), 1)
    parts = [column == lane + start for start in range(0, count, 128)]
    return jnp.concatenate([p.astype(jnp.float32) for p in parts], axis=1).astype(jnp.bfloat16)


def place_rows(order):
    count = order.shape[1]
    row = lax.broadcasted_iota(jnp.int32, (count, count), 0)
    return (row == order).astype(jnp.float32).astype(jnp.bfloat16)


def local_order(order_ref):
    return jnp.bitwise_and(order_ref[...], order_ref.shape[1] - 1)


def add_bias(scores, lists_ref, first_query, first_key):
    parts = []
    for at in range(scores.shape[0] // TILE_POINTS):
        bias = []
        for query in range(scores.shape[1] // TILE_POINTS):
            slot = first_key + at - first_query - query + BAND
            listed = lists_ref[first_query + query, jnp.clip(slot, 0, 2 * BAND)] >= 0
            admitted = listed & (slot >= 0) & (slot <= 2 * BAND)
            value = jnp.where(admitted, 0.0, MASKED).astype(jnp.float32)
            bias.append(jnp.full((1, TILE_POINTS), value, jnp.float32))
        rows = scores[at * TILE_POINTS : (at + 1) * TILE_POINTS]
        parts.append(rows + jnp.concatenate(bias, axis=1))
    return jnp.concatenate(parts, axis=0)


def exp_of(scores, peak):
    return jnp.exp2((scores - peak) * EXP_SCALE)


def peak_of(scores):
    return jnp.max(scores, axis=0, keepdims=True)


def total_of(weights):
    return jnp.sum(weights, axis=0, keepdims=True)


def columns_of(head):
    return slice(head * HEAD_WIDTH, (head + 1) * HEAD_WIDTH)


def in_lower_half():
    return lax.axis_index("grp") < lax.axis_size("grp") // 2


def sort_kernel(lists_hbm, order_hbm, k_hbm, v_hbm, kv_hbm, outward, inward, first_out, second_out, *rest):
    pieces = rest[:-7]
    lists_ref, order_ref, unsorted, sorted_kv, arrived, left, small = rest[-7:]
    count, width = k_hbm.shape
    order_copy = pltpu.make_async_copy(order_hbm, order_ref, small.at[0])
    lists_copy = pltpu.make_async_copy(lists_hbm, lists_ref, small.at[1])
    order_copy.start()
    lists_copy.start()
    copies = []
    for which, ref in enumerate((k_hbm, v_hbm)):
        for start in range(0, count, TILE_POINTS):
            rows = pl.ds(start, TILE_POINTS)
            done = arrived.at[which, start // TILE_POINTS]
            copies.append(pltpu.make_async_copy(ref.at[rows], unsorted.at[which, rows], done))
    for copy in copies:
        copy.start()
    order_copy.wait()
    pick = pick_rows(local_order(order_ref))
    lists_copy.wait()
    tile = lax.rem(lists_ref[0, 2 * BAND + 1], count // TILE_POINTS)
    mine = lax.rem(lax.axis_index("blk"), len(pieces))
    piece_rows = TILE_POINTS // len(pieces)
    low, high = 0, count - HALO
    outward_first = lax.rem(lax.axis_index("blk"), 2) == 0
    out_start = jnp.where(in_lower_half(), low, high)
    in_start = jnp.where(in_lower_half(), high, low)
    out_rows = pl.ds(pl.multiple_of(out_start, HALO), HALO)
    in_rows = pl.ds(pl.multiple_of(in_start, HALO), HALO)
    first_rows = pl.ds(pl.multiple_of(jnp.where(outward_first, out_start, in_start), HALO), HALO)
    second_rows = pl.ds(pl.multiple_of(jnp.where(outward_first, in_start, out_start), HALO), HALO)
    leaving = []
    for which in range(2):
        for copy in copies[which * len(copies) // 2 : (which + 1) * len(copies) // 2]:
            copy.wait()
        for start in range(0, width, PAIR):
            cols = pl.ds(start, PAIR)
            rows = mm(pick, unsorted[which, :, start : start + PAIR]).astype(jnp.bfloat16)
            sorted_kv[which, :, start : start + PAIR] = rows
            targets = [
                (slice(None), kv_hbm.at[which, :, cols]),
                (out_rows, outward.at[which, :, cols]),
                (in_rows, inward.at[which, :, cols]),
                (first_rows, first_out.at[which, :, cols]),
                (second_rows, second_out.at[which, :, cols]),
            ]
            for step, piece_ref in enumerate(pieces):
                first = tile * TILE_POINTS + lax.rem(mine + step, len(pieces)) * piece_rows
                first = pl.multiple_of(first, piece_rows)
                targets.append((pl.ds(first, piece_rows), piece_ref.at[which, :, cols]))
            for number, (taken, target) in enumerate(targets):
                done = left.at[which, start // PAIR, number]
                copy = pltpu.make_async_copy(sorted_kv.at[which, taken, cols], target, done)
                copy.start()
                leaving.append(copy)
    for copy in leaving:
        copy.wait()


def select_kernel(rule, lists_ref, got_ref, held_ref, out_ref):
    out_ref[...] = jnp.where(rule(lists_ref[0, 2 * BAND + 1]), got_ref[...], held_ref[...])


def query_kernel(order_ref, q_ref, qs_ref, place_ref, pick):
    @pl.when(pl.program_id(0) == 0)
    def _():
        order = local_order(order_ref)
        place_ref[...] = place_rows(order)
        pick[...] = pick_rows(order)

    qs_ref[...] = mm(pick[...], q_ref[...]).astype(jnp.bfloat16)


def own_kernel(lists_ref, qs_ref, kv_ref, acc_ref, ml_ref):
    for at in range(PAIR_HEADS):
        cols = columns_of(at)
        scores = add_bias(mm_nt(kv_ref[0, :, cols], qs_ref[:, cols]), lists_ref, 0, 0)
        peak = peak_of(scores)
        weights = exp_of(scores, peak)
        ml_ref[at : at + 1] = peak
        ml_ref[PAIR_HEADS + at : PAIR_HEADS + at + 1] = total_of(weights)
        acc_ref[cols] = mm_tn(kv_ref[1, :, cols], weights.astype(jnp.bfloat16))


def halo_place(is_low, count):
    tiles = count // TILE_POINTS
    start = pl.multiple_of(jnp.where(is_low, 0, count - HALO), HALO)
    return start, jnp.where(is_low, 0, tiles - BAND), jnp.where(is_low, -BAND, tiles)


def take_keys(old, scores, values, summed):
    old_peak, old_total = old
    peak = jnp.maximum(old_peak, peak_of(scores))
    shrink = exp_of(old_peak, peak)
    weights = exp_of(scores, peak)
    total = old_total * shrink + total_of(weights)
    return peak, total, summed * shrink + mm_tn(values, weights.astype(jnp.bfloat16))


def at_middle():
    here, middle = lax.axis_index("grp"), lax.axis_size("grp") // 2
    return (here == middle) | (here == middle - 1)


def meets_early():
    return at_middle() == (lax.rem(lax.axis_index("blk"), 2) == 1)


def near_kernel(lists_ref, qs_ref, near_kv, acc_ref, ml_ref, new_acc_ref, new_ml_ref):
    new_acc_ref[...] = acc_ref[...]
    new_ml_ref[...] = ml_ref[...]

    @pl.when(meets_early())
    def _():
        start, first_query, first_key = halo_place(jnp.logical_not(in_lower_half()), qs_ref.shape[0])
        met = pl.ds(start, HALO)
        for at in range(PAIR_HEADS):
            cols = columns_of(at)
            scores = mm_nt(near_kv[0, :, cols], qs_ref[met, cols])
            scores = add_bias(scores, lists_ref, first_query, first_key)
            old = ml_ref[at : at + 1, met], ml_ref[PAIR_HEADS + at : PAIR_HEADS + at + 1, met]
            peak, total, summed = take_keys(old, scores, near_kv[1, :, cols], acc_ref[cols, met])
            new_acc_ref[cols, met] = summed
            new_ml_ref[at : at + 1, met] = peak
            new_ml_ref[PAIR_HEADS + at : PAIR_HEADS + at + 1, met] = total


def global_kernel(lists_ref, qs_ref, acc_ref, ml_ref, *rest):
    pieces, (new_acc_ref, new_ml_ref) = rest[:-2], rest[-2:]
    for at in range(PAIR_HEADS):
        cols = columns_of(at)
        old = ml_ref[at : at + 1], ml_ref[PAIR_HEADS + at : PAIR_HEADS + at + 1]
        keys = jnp.concatenate([ref[0, :, cols] for ref in pieces], axis=0)
        values = jnp.concatenate([ref[1, :, cols] for ref in pieces], axis=0)
        peak, total, summed = take_keys(old, mm_nt(keys, qs_ref[:, cols]), values, acc_ref[cols])
        new_acc_ref[cols] = summed
        new_ml_ref[at : at + 1] = peak
        new_ml_ref[PAIR_HEADS + at : PAIR_HEADS + at + 1] = total


def finish_kernel(lists_ref, place_ref, qs_ref, acc_ref, ml_ref, *rest):
    next_kv, late_kv, even_kv, odd_kv, out_ref, attended, halos, arrived = rest
    count = qs_ref.shape[0]
    here, end = lax.axis_index("grp"), lax.axis_size("grp") - 1
    at_end = (here == 0) | (here == end)
    even_wrap = (lax.rem(lax.axis_index("blk"), 2) == 0) == (here == end)
    sources = (
        (jnp.logical_not(at_end), 0, next_kv),
        (at_end & even_wrap, 0, even_kv),
        (at_end & jnp.logical_not(even_wrap), 0, odd_kv),
        (jnp.logical_not(meets_early()), 1, late_kv),
    )
    step = pl.program_id(0)

    @pl.when(step == 0)
    def _():
        copies = []
        for chosen, side, source in sources:
            pieces = [
                pltpu.make_async_copy(source.at[w], halos.at[side, w], arrived.at[side, w]) for w in range(2)
            ]
            copies.append((chosen, pieces))

            @pl.when(chosen)
            def _():
                for copy in pieces:
                    copy.start()

        for chosen, pieces in copies:

            @pl.when(chosen)
            def _():
                for copy in pieces:
                    copy.wait()

    def add_halo(side, is_low):
        start, first_query, first_key = halo_place(is_low, count)
        met = pl.ds(start, HALO)
        for at in range(PAIR_HEADS):
            cols = columns_of(at)
            here_cols = pl.ds(pl.multiple_of(step * PAIR + at * HEAD_WIDTH, HEAD_WIDTH), HEAD_WIDTH)
            scores = mm_nt(halos[side, 0, :, here_cols], qs_ref[met, cols])
            scores = add_bias(scores, lists_ref, first_query, first_key)
            old = ml_ref[at : at + 1, met], ml_ref[PAIR_HEADS + at : PAIR_HEADS + at + 1, met]
            _, total, summed = take_keys(old, scores, halos[side, 1, :, here_cols], acc_ref[cols, met])
            attended[cols, met] = (summed / total).astype(jnp.bfloat16)

    add_halo(0, in_lower_half())

    @pl.when(jnp.logical_not(meets_early()))
    def _():
        add_halo(1, jnp.logical_not(in_lower_half()))

    @pl.when(meets_early())
    def _():
        start, _, _ = halo_place(jnp.logical_not(in_lower_half()), count)
        left = pl.ds(start, HALO)
        for at in range(PAIR_HEADS):
            cols = columns_of(at)
            total = ml_ref[PAIR_HEADS + at : PAIR_HEADS + at + 1, left]
            attended[cols, left] = (acc_ref[cols, left] / total).astype(jnp.bfloat16)

    out_ref[...] = mm_nt(place_ref[...], attended[...]).astype(jnp.bfloat16)


def join_kernel(first, second, joined):
    rows = first.shape[1]
    joined[:, :rows] = first[...]
    joined[:, rows:] = second[...]


SMEM = pl.BlockSpec(memory_space=pltpu.SMEM)
VMEM = pl.BlockSpec(memory_space=pltpu.VMEM)
HBM = pl.BlockSpec(memory_space=pltpu.HBM)
ANY = pl.BlockSpec(memory_space=pl.ANY)
SORT_LIMIT = VMEM_LIMIT
LONG = 20000000000


def column_block(*leading):
    zeros = (0,) * len(leading)
    return pl.BlockSpec((*leading, PAIR), lambda i: (*zeros, i))


def row_block(rows, width):
    return pl.BlockSpec((rows, width), lambda i: (i, 0))


def whole_block(*shape):
    return pl.BlockSpec(shape, lambda i: (0,) * len(shape))


def spread_rounds(axis):
    count = lax.axis_size(axis)
    middle = count // 2

    def round_of(pairs, low_end, high_start):
        (_, upper), (_, lower) = pairs

        def rule(root):
            at = lax.axis_index(axis)
            return ((at == upper) & (root < low_end)) | ((at == lower) & (root >= high_start))

        return pairs, rule

    rounds = []
    for i in range(middle - 1):
        rounds.append(round_of([(i, i + 1), (count - 1 - i, count - 2 - i)], i + 1, count - 1 - i))
    rounds.append(round_of([(middle - 1, middle), (middle, middle - 1)], middle, middle))
    for i in range(middle - 1, 0, -1):
        rounds.append(round_of([(count - 1 - i, count - i), (i, i - 1)], count - i, i))
    return rounds


def body(query_rows, key_rows, value_rows, tile_lists, hilbert_order):
    row_count, feature_count = query_rows.shape
    tiles_here = row_count // TILE_POINTS
    blk_count, grp_count = lax.axis_size("blk"), lax.axis_size("grp")
    part = blk_count // NG
    bf16 = functools.partial(jax.ShapeDtypeStruct, dtype=jnp.bfloat16)
    f32 = functools.partial(jax.ShapeDtypeStruct, dtype=jnp.float32)

    def in_hbm(*arrays):
        return [pltpu.with_memory_space_constraint(array, pltpu.HBM) for array in arrays]

    def call(kernel, name, ins, outs, out_shape, scratch=(), cost=None, grid=(), limit=VMEM_LIMIT):
        return pl.pallas_call(
            kernel,
            grid=grid,
            in_specs=ins,
            out_specs=outs,
            out_shape=out_shape,
            scratch_shapes=scratch,
            cost_estimate=cost,
            compiler_params=pltpu.CompilerParams(vmem_limit_bytes=limit),
            name=name,
        )

    order = hilbert_order.reshape(1, row_count)
    piece_rows = TILE_POINTS // part
    halo = bf16((2, HALO, feature_count))
    kv, outward, inward, first_out, second_out, *pieces = call(
        sort_kernel,
        "sort_keys_values",
        [HBM] * 4,
        [ANY] * (5 + part),
        [bf16((2, row_count, feature_count)), *[halo] * 4]
        + [bf16((2, piece_rows, feature_count))] * part,
        [
            pltpu.SMEM(tile_lists.shape, jnp.int32),
            pltpu.VMEM((1, row_count), jnp.int32),
            pltpu.VMEM((2, row_count, feature_count), jnp.bfloat16),
            pltpu.VMEM((2, row_count, feature_count), jnp.bfloat16),
            pltpu.SemaphoreType.DMA((2, tiles_here)),
            pltpu.SemaphoreType.DMA((2, feature_count // PAIR, 5 + part)),
            pltpu.SemaphoreType.DMA((2,)),
        ],
        limit=SORT_LIMIT,
    )(tile_lists, order, *in_hbm(key_rows, value_rows))

    def owner_of(tile_id):
        owner = lax.div(lax.rem(tile_id, tiles_here * blk_count * grp_count // NG), tiles_here)
        return lax.div(owner, grp_count), lax.rem(owner, grp_count)

    def select(rule, got, held, flops=1):
        return call(
            functools.partial(select_kernel, rule),
            "select_piece",
            [SMEM] + [VMEM] * 2,
            VMEM,
            bf16(held.shape),
            cost=pl.CostEstimate(flops=flops, bytes_accessed=flops, transcendentals=0),
        )(tile_lists, got, held)

    middle = grp_count // 2
    away = [(i, i - 1) for i in range(1, middle)] + [(i, i + 1) for i in range(middle, grp_count - 1)]
    towards = [(target, source) for source, target in away]
    across = [(middle - 1, middle), (middle, middle - 1)]

    def exchange(turn):
        links = []
        for run in range(blk_count):
            chosen = (away, across)[(run + turn) % 2]
            links += [(run * grp_count + i, run * grp_count + j) for i, j in chosen]
        return links

    wraps = [[], []]
    for run in range(1, blk_count):
        first = run * grp_count
        wraps[(run + 1) % 2] += [(first - 1, first), (first, first - 1)]
    tie = lax.optimization_barrier
    rounds = spread_rounds("grp")
    inner = middle - 1
    listed = tile_lists[0, 2 * BAND + 1] >= 0

    def stage(run, *operands):
        shapes = jax.eval_shape(run, *operands)
        skip = lambda *_: jax.tree.map(lambda leaf: jnp.zeros(leaf.shape, leaf.dtype), shapes)
        return lax.cond(listed, run, skip, *operands)

    def send(piece, some):
        for pairs, rule in some[:-1]:
            piece = take(rule, lax.ppermute(piece, "grp", pairs), piece)
        return piece, lax.ppermute(piece, "grp", some[-1][0])

    def take(rule, got, piece, **cost):
        return select(lambda tile_id: rule(owner_of(tile_id)[1]), got, piece, **cost)

    grid = (feature_count // PAIR,)
    idle = pl.CostEstimate(flops=1, bytes_accessed=1, transcendentals=0)
    busy = pl.CostEstimate(flops=LONG, bytes_accessed=LONG, transcendentals=0)
    queries_block = column_block(row_count)
    state_blocks = [row_block(PAIR, row_count), row_block(STATE_ROWS, row_count)]
    state_shapes = [f32((feature_count, row_count)), f32((grid[0] * STATE_ROWS, row_count))]
    inward_rounds, across_round, outward_rounds = rounds[:inner], rounds[inner], rounds[inner + 1 :]

    def inward_stage(piece):
        queries, place = call(
            query_kernel,
            "sort_queries",
            [whole_block(1, row_count), queries_block],
            [queries_block, whole_block(row_count, row_count)],
            [bf16((row_count, feature_count)), bf16((row_count, row_count))],
            [pltpu.VMEM((row_count, row_count), jnp.bfloat16)],
            cost=busy,
            grid=grid,
        )(order, query_rows)
        return *send(piece, inward_rounds), queries, place

    def across_stage(piece, kv, queries):
        own = call(
            own_kernel,
            "attend_own",
            [SMEM, queries_block, column_block(2, row_count)],
            state_blocks,
            state_shapes,
            cost=busy,
            grid=grid,
        )(tile_lists, queries, kv)
        piece, got = send(piece, [across_round])
        return take(across_round[1], got, piece), own

    def outward_stage(piece, outward, second_out, queries, own, near_kv):
        late_kv = lax.ppermute(second_out, ("blk", "grp"), exchange(1))
        own = call(
            near_kernel,
            "attend_near",
            [SMEM, queries_block, column_block(2, HALO)] + state_blocks,
            state_blocks,
            state_shapes,
            cost=busy,
            grid=grid,
        )(tile_lists, queries, near_kv, *own)
        piece, got = send(piece, outward_rounds)
        got, outward = tie((got, outward))
        even_kv = lax.ppermute(outward, ("blk", "grp"), wraps[0])
        piece = take(outward_rounds[-1][1], got, piece, flops=LONG)
        states, odd_kv = stage(plane_stage, piece, outward, queries, own)
        return states, late_kv, even_kv, odd_kv

    def plane_stage(piece, outward, queries, own):
        for step in range(2):
            turns = [1 if i % part % 2 == step else 2 for i in range(blk_count)]
            links = [(i, (i // part ^ turn) * part + i % part) for i, turn in enumerate(turns)]
            got = lax.ppermute(piece, "blk", links)
            if step == 1:
                got, outward = tie((got, outward))
                odd_kv = lax.ppermute(outward, ("blk", "grp"), wraps[1])
            rows = 2 * piece.shape[1]
            joined = bf16((2, rows, feature_count))
            cost = (idle, busy)[step]
            piece = call(join_kernel, "join_pieces", [VMEM] * 2, VMEM, joined, cost=cost)(piece, got)
        return stage(global_stage, piece, queries, own), odd_kv

    def global_stage(quarters, queries, own):
        pieces = [quarters]
        for step in range(1, part):
            pairs = [(i, i // part * part + (i + step) % part) for i in range(blk_count)]
            pieces.append(lax.ppermute(quarters, "blk", pairs))
        return call(
            global_kernel,
            "attend_global",
            [SMEM, queries_block] + state_blocks + [column_block(2, NG * piece_rows)] * part,
            state_blocks,
            state_shapes,
            cost=idle,
            grid=grid,
        )(tile_lists, queries, *own, *pieces)

    near_kv = lax.ppermute(first_out, ("blk", "grp"), exchange(0))
    piece = pieces[0]
    for step in range(1, part):
        pairs = [(i, i // part * part + (i + step) % part) for i in range(blk_count)]
        got = lax.ppermute(pieces[step], "blk", pairs)

        def from_owner(tile_id, step=step):
            return lax.rem(lax.axis_index("blk") + part - step, part) == owner_of(tile_id)[0]

        piece = select(from_owner, got, piece, flops=LONG)
    piece, got, queries, place = stage(inward_stage, piece)
    got, inward = tie((got, inward))
    next_kv = lax.ppermute(inward, "grp", towards)
    piece = take(inward_rounds[-1][1], got, piece)
    piece, own = stage(across_stage, piece, kv, queries)
    piece, near_kv = tie((piece, near_kv))
    states, late_kv, even_kv, odd_kv = stage(outward_stage, piece, outward, second_out, queries, own, near_kv)
    return call(
        finish_kernel,
        "attend_last",
        [SMEM, whole_block(row_count, row_count), queries_block] + state_blocks + [ANY] * 4,
        queries_block,
        bf16((row_count, feature_count)),
        [
            pltpu.VMEM((PAIR, row_count), jnp.bfloat16),
            pltpu.VMEM((2, 2, HALO, feature_count), jnp.bfloat16),
            pltpu.SemaphoreType.DMA((2, 2)),
        ],
        grid=grid,
    )(tile_lists, place, queries, *states, next_kv, late_kv, even_kv, odd_kv)


def solution(mesh):
    rows = P(("blk", "grp"), None)
    in_specs = (rows, rows, rows, rows, P(("blk", "grp")))
    return jax.shard_map(body, mesh=mesh, in_specs=in_specs, out_specs=rows, check_vma=False)
```

time: 351 us -> 90.1 us (0.26)
  waiting for transfers between devices: 151 us -> 30.4 us
  local copies, waits for them, and re-layouts: 102 us -> 1.22 us
  matrix products: 48.7 us -> 0 us
  Pallas kernels: 0 us -> 36.1 us
  between operations: 23.6 us -> 0.68 us
  starting transfers between devices: 9.33 us -> 21.2 us
  other arithmetic: 10.1 us -> 0 us
    psum x1 -> x0, waiting for transfers between devices: 151 us -> none  [spread(): return lax.psum(jnp.where(mine, array, jnp.zeros_like(array)), axis)]
    dot_general x8 -> x0, matrix products: 38.4 us -> none  [the longest x4 26.4 us: one_tile(): jnp.einsum('hqk,khd->qhd', weights, value_heads, preferred_element_type=j...]
    dynamic_slice x16 -> x0, local copies, waits for them, and re-layouts: 38.1 us -> none  [the longest x8 31.9 us: one_tile(): lax.dynamic_slice_in_dim(padded, tile_number * TILE_POINTS, (2 * BAND + 1...]
    pallas_call x0 -> x12, Pallas kernels: none -> 36.1 us  [the longest x1 7.62 us: body(): call(finish_kernel, 'attend_last', [SMEM, whole_block(row_count, row_coun...]
    while x28 -> x0, local copies, waits for them, and re-layouts: 32.4 us -> none
    ppermute x2 -> x12, waiting for transfers between devices: 0.01 us -> 30.4 us  [the longest x2 14 us: plane_stage(): got = lax.ppermute(piece, 'blk', links)]
    ppermute x2 -> x12, starting transfers between devices: 9.33 us -> 21.2 us  [the longest x3 8.2 us: send(): return (piece, lax.ppermute(piece, 'grp', some[-1][0]))]
    sub x4 -> x0, matrix products: 10.3 us -> none  [one_tile(): exponent = jnp.exp(scores - row_peak)]
  transfers between devices with their start and end apart: 3 -> 12, of which waited for: 1 -> 6; matrix products, arithmetic and copies ran while one was open for 5% -> 1% of each run, Pallas kernels for 0% -> 27%
where the time goes in v2:
time: 90.1 us; the launch traced here: 89.7 us
  Pallas kernels  36.1 us (40%)
  waiting for transfers between devices  30.4 us (34%)
  starting transfers between devices  21.2 us (24%)
  local copies, waits for them, and re-layouts  1.22 us (1%)
    ppermute x2, waiting for transfers between devices, plane_stage(): got = lax.ppermute(piece, 'blk', links)  14 us
    ppermute x3, starting transfers between devices, send(): return (piece, lax.ppermute(piece, 'grp', some[-1][0]))  8.2 us
    pallas_call x1, Pallas kernels, body(): call(finish_kernel, 'attend_last', [SMEM, whole_block(row_count, row_coun...  7.62 us
    ppermute x1, waiting for transfers between devices, plane_stage(): odd_kv = lax.ppermute(outward, ('blk', 'grp'), wraps[1])  7.2 us
    pallas_call x1, Pallas kernels, global_stage(): call(global_kernel, 'attend_global', [SMEM, queries_block] + state_blocks...  7 us
    ppermute x3, waiting for transfers between devices, send(): return (piece, lax.ppermute(piece, 'grp', some[-1][0]))  6.36 us
    pallas_call x1, Pallas kernels, across_stage(): call(own_kernel, 'attend_own', [SMEM, queries_block, column_block(2, row_...  5.87 us
    pallas_call x1, Pallas kernels, outward_stage(): call(near_kernel, 'attend_near', [SMEM, queries_block, column_block(2, HA...  4.9 us
  transfers between devices with their start and end apart: 12, of which 6 were waited for; matrix products, arithmetic and copies ran while one was open for 1% of the time, Pallas kernels for 27%

profile of v2, /device:TPU:4, one launch (start us, length us, event | category | flops | bytes accessed | tf_op | source)
XLA Modules:
  0.0 89.7 jit_solution(298989055493969043)
XLA Ops:
  0.0 4.6 %sort_keys_values.1 = (bf16[2,512,1024]{2,1,0:T(8,128)(2,1)}, bf16[2,256,1024]{2,1,0:T(8,128)(2,1)}, bf16[2,256,1024]{2,1,0:T(8,128)(2,1)S(1)}, bf16[2,256,1024]...) custom-call(s32[4,9]{1,0:T(4,128)} %lists_ref.5, ...), custom_call_target="tpu_custom_call" | custom-call | tf_op jit(solution)/shard_map/sort_keys_values/pallas_call | solution.py:369
  4.7 1.3 %collective-permute-start.10 = (bf16[2,256,1024]{2,1,0:T(8,128)(2,1)}, bf16[2,256,1024]{2,1,0:T(8,128)(2,1)}, u32[]{:S(2)}, u32[]{:S(2)}) collective-permute-start(bf16[2,256,1024]{2,1,0:T(8,128)(2,1)} %get-tuple-element.137), channel_id=1, source_target_pairs={{1,0},{2,3},{5,6},{6,5},{9,8},{10,11},{13,14},{14,13},{17,16},{18,... | collective-permute-start | bytes 3145736 | tf_op jit(solution)/shard_map/ppermute | solution.py:517
  6.0 0.6 slice.3
  7.2 0.6 select_piece.6
  8.5 11.6 %conditional.5 = (bf16[2,64,1024]{2,1,0:T(8,128)(2,1)S(1)}, bf16[2,64,1024]{2,1,0:T(8,128)(2,1)}, bf16[512,1024]{1,0:T(8,128)(2,1)}, bf16[512,512]{1,0:T(8,128)(2,1)}) conditional(s32[]{:T(128)} %convert_element_type.11, () %tuple.48, (bf16[2,64,1024]{2,1,0:T(8,128)(2,1)S(1)}, s32[1,512]{1,0:T(1,128)S(1)}, bf16[512,1024]{1,0:T(8,128)(2,1)S(1)}) %tuple.71), branch_computations={%region_0.0_spmd, %region_1.0_spmd} | conditional | flops 20000000000 | bytes 20001572864 | solution.py:426
  8.5 6.2 %collective-permute-start = (bf16[2,64,1024]{2,1,0:T(8,128)(2,1)S(1)}, bf16[2,64,1024]{2,1,0:T(8,128)(2,1)}, u32[]{:S(2)}, u32[]{:S(2)}) collective-permute-start(bf16[2,64,1024]{2,1,0:T(8,128)(2,1)S(1)} %get-tuple-element.166), channel_id=1, source_target_pairs={{0,1},{3,2},{4,5},{7,6},{8,9},{11,10},{12,13},{15,14},{16,17},{19,... | collective-permute-start | bytes 786440 | tf_op jit(solution)/shard_map/cond/branch_1_fun/ppermute | solution.py:431
  14.7 2.2 %sort_queries.1 = (bf16[512,1024]{1,0:T(8,128)(2,1)}, bf16[512,512]{1,0:T(8,128)(2,1)}) custom-call(s32[1,512]{1,0:T(1,128)S(1)} %get-tuple-element.62.order_ref, bf16[512,1024]{1,0:T(8,128)(2,1)S(1)} %get-tuple-element.151.q_ref), custom_call_target="tpu_custom_call" | custom-call | flops 20000000000 | bytes 20000000000 | tf_op jit(solution)/shard_map/cond/branch_1_fun/sort_queries/pallas_call | solution.py:445
  16.9 3.2 %collective-permute-done = bf16[2,64,1024]{2,1,0:T(8,128)(2,1)} collective-permute-done((bf16[2,64,1024]{2,1,0:T(8,128)(2,1)S(1)}, bf16[2,64,1024]{2,1,0:T(8,128)(2,1)}, u32[]{:S(2)}, u32[]{:S(2)}) %collective-permute-start) | collective-permute-done | bytes 262176 | tf_op jit(solution)/shard_map/cond/branch_1_fun/ppermute | solution.py:431
  20.1 4.5 %collective-permute-start.11 = (bf16[2,256,1024]{2,1,0:T(8,128)(2,1)S(1)}, bf16[2,256,1024]{2,1,0:T(8,128)(2,1)S(1)}, u32[]{:S(2)}, u32[]{:S(2)}) collective-permute-start(bf16[2,256,1024]{2,1,0:T(8,128)(2,1)S(1)} %get-tuple-element.146), channel_id=1, source_target_pairs={{0,1},{3,2},{4,5},{7,6},{8,9},{11,10},{12,13},{15,14},{16,17},{19,... | collective-permute-start | bytes 3145736 | tf_op jit(solution)/shard_map/ppermute | solution.py:529
  24.6 1.0 %select_piece.7 = bf16[2,64,1024]{2,1,0:T(8,128)(2,1)S(1)} custom-call(s32[4,9]{1,0:T(4,128)S(1)} %copy-done, bf16[2,64,1024]{2,1,0:T(8,128)(2,1)} %get-tuple-element.133.got_ref, bf16[2,64,1024]{2,1,0:T(8,128)(2,1)S(1)} %get-tuple-element.134.held_ref), custom_call_target="tpu_custom_call" | custom-call | flops 1 | bytes 1 | tf_op jit(solution)/shard_map/select_piece/pallas_call | solution.py:393
  25.6 7.2 %conditional.6 = (bf16[2,64,1024]{2,1,0:T(8,128)(2,1)S(1)}, f32[1024,512]{1,0:T(8,128)S(1)}, f32[16,512]{1,0:T(8,128)S(1)}) conditional(s32[]{:T(128)} %convert_element_type.11, () %tuple.51, (bf16[2,64,1024]{2,1,0:T(8,128)(2,1)S(1)}, s32[4,9]{1,0:T(4,128)S(1)}, bf16[512,1024]{1,0:T(8,128)(2,1)}, bf16[2,512,1024]{2,1,0:T(8,128)(2,1)}) %tuple.68), branch_computations={%region_2.0_spmd, %region_3.0_spmd} | conditional | flops 20000000000 | bytes 20001048576 | solution.py:426
  25.6 0.7 collective-permute-start.1
  26.3 5.9 %attend_own.1 = (f32[1024,512]{1,0:T(8,128)S(1)}, f32[16,512]{1,0:T(8,128)S(1)}) custom-call(s32[4,9]{1,0:T(4,128)S(1)} %get-tuple-element.66.lists_ref, bf16[512,1024]{1,0:T(8,128)(2,1)} %get-tuple-element.68.qs_ref, bf16[2,512,1024]{2,1,0:T(8,128)(2,1)} %get-tuple-element.69.kv_ref), custom_call_target="tpu_custom_call" | custom-call | flops 20000000000 | bytes 20000000000 | tf_op jit(solution)/shard_map/cond/branch_1_fun/attend_own/pallas_call | solution.py:458
  32.2 0.6 select_piece.4
  32.8 49.2 %conditional.7 = (f32[1024,512]{1,0:T(8,128)}, f32[16,512]{1,0:T(8,128)}, bf16[2,256,1024]{2,1,0:T(8,128)(2,1)}, bf16[2,256,1024]{2,1,0:T(8,128)(2,1)}, bf16[2,256,1024]{2,1,0:T(8,128)(2,1)}) conditional(s32[]{:T(128)} %convert_element_type.11, () %tuple.50, (pred[]{:T(512)}, bf16[2,64,1024]{2,1,0:T(8,128)(2,1)S(1)}, bf16[2,256,1024]{2,1,0:T(8,128)(2,1)}, ...), branch_computations={%region_4.0_spmd, %region_5.0_spmd} | conditional | flops 60000002048 | bytes 60020973568 | solution.py:426
  32.8 1.3 %collective-permute-start.6 = (bf16[2,64,1024]{2,1,0:T(8,128)(2,1)S(1)}, bf16[2,64,1024]{2,1,0:T(8,128)(2,1)S(1)}, u32[]{:S(2)}, u32[]{:S(2)}) collective-permute-start(bf16[2,64,1024]{2,1,0:T(8,128)(2,1)S(1)} %get-tuple-element.90.held_ref), channel_id=1, source_target_pairs={{2,3},{1,0},{6,7},{5,4},{10,11},{9,8},{14,15},{13,12},{18,19},{17,... | collective-permute-start | bytes 786440 | tf_op jit(solution)/shard_map/cond/branch_1_fun/ppermute | solution.py:431
  34.1 1.8 %collective-permute-start.7 = (bf16[2,256,1024]{2,1,0:T(8,128)(2,1)}, bf16[2,256,1024]{2,1,0:T(8,128)(2,1)}, u32[]{:S(2)}, u32[]{:S(2)}) collective-permute-start(bf16[2,256,1024]{2,1,0:T(8,128)(2,1)} %get-tuple-element.102), channel_id=1, source_target_pairs={{1,2},{2,1},{5,4},{6,7},{9,10},{10,9},{13,12},{14,15},{17,18},{18,... | collective-permute-start | bytes 3145736 | tf_op jit(solution)/shard_map/cond/branch_1_fun/ppermute | solution.py:471
  35.9 4.9 %attend_near.1 = (f32[1024,512]{1,0:T(8,128)}, f32[16,512]{1,0:T(8,128)S(1)}) custom-call(s32[4,9]{1,0:T(4,128)S(1)} %get-tuple-element.89.lists_ref, bf16[512,1024]{1,0:T(8,128)(2,1)} %get-tuple-element.94.qs_ref, bf16[2,256,1024]{2,1,0:T(8,128)(2,1)} %get-tuple-element.95.near_kv, f32[1024,512]{1,0:T(8,128)S(1)} %get-tuple-element.96.acc_ref, ...), custom_call_target="tpu_custom_call" | custom-call | flops 20000000000 | bytes 20000000000 | tf_op jit(solution)/shard_map/cond/branch_1_fun/attend_near/pallas_call | solution.py:472
  40.8 3.2 %collective-permute-done.6.got_ref = bf16[2,64,1024]{2,1,0:T(8,128)(2,1)S(1)} collective-permute-done((bf16[2,64,1024]{2,1,0:T(8,128)(2,1)S(1)}, bf16[2,64,1024]{2,1,0:T(8,128)(2,1)S(1)}, u32[]{:S(2)}, u32[]{:S(2)}) %collective-permute-start.6) | collective-permute-done | bytes 262176 | tf_op jit(solution)/shard_map/cond/branch_1_fun/ppermute | solution.py:431
  44.0 1.7 %collective-permute-start.8 = (bf16[2,256,1024]{2,1,0:T(8,128)(2,1)}, bf16[2,256,1024]{2,1,0:T(8,128)(2,1)}, u32[]{:S(2)}, u32[]{:S(2)}) collective-permute-start(bf16[2,256,1024]{2,1,0:T(8,128)(2,1)} %get-tuple-element.93), channel_id=1, source_target_pairs={{3,4},{4,3},{11,12},{12,11},{19,20},{20,19},{27,28},{28,27}} | collective-permute-start | bytes 3145736 | tf_op jit(solution)/shard_map/cond/branch_1_fun/ppermute | solution.py:483
  45.7 0.6 select_piece.5
  46.3 35.8 %conditional.1 = (f32[1024,512]{1,0:T(8,128)}, f32[16,512]{1,0:T(8,128)}, bf16[2,256,1024]{2,1,0:T(8,128)(2,1)}) conditional(s32[]{:T(128)} %convert_element_type.2, () %tuple.36, (pred[]{:T(512)}, bf16[2,64,1024]{2,1,0:T(8,128)(2,1)S(1)}, bf16[2,256,1024]{2,1,0:T(8,128)(2,1)}, s32[4,9]{1,0:T(4,128)S(1)}, bf16[512,1024]{1,0:T(8,128)(2,1)}, ...), branch_computations={%region_6.0_spmd, %region_7.0_spmd} | conditional | flops 20000000000 | bytes 20011534336 | solution.py:426
  46.3 1.6 %collective-permute-start.3 = (bf16[2,64,1024]{2,1,0:T(8,128)(2,1)S(1)}, bf16[2,64,1024]{2,1,0:T(8,128)(2,1)S(1)}, u32[]{:S(2)}, u32[]{:S(2)}) collective-permute-start(bf16[2,64,1024]{2,1,0:T(8,128)(2,1)S(1)} %get-tuple-element.78.first), channel_id=1, source_target_pairs={{0,8},{4,20},{8,0},{12,28},{16,24},{20,4},{24,16},{28,12},{1,9},{5... | collective-permute-start | bytes 786440 | tf_op jit(solution)/shard_map/cond/branch_1_fun/cond/branch_1_fun/ppermute | solution.py:492
  47.9 4.9 %collective-permute-done.3.second = bf16[2,64,1024]{2,1,0:T(8,128)(2,1)S(1)} collective-permute-done((bf16[2,64,1024]{2,1,0:T(8,128)(2,1)S(1)}, bf16[2,64,1024]{2,1,0:T(8,128)(2,1)S(1)}, u32[]{:S(2)}, u32[]{:S(2)}) %collective-permute-start.3) | collective-permute-done | bytes 262176 | tf_op jit(solution)/shard_map/cond/branch_1_fun/cond/branch_1_fun/ppermute | solution.py:492
  53.0 9.1 %collective-permute-done.4.second = bf16[2,128,1024]{2,1,0:T(8,128)(2,1)S(1)} collective-permute-done((bf16[2,128,1024]{2,1,0:T(8,128)(2,1)S(1)}, bf16[2,128,1024]{2,1,0:T(8,128)(2,1)S(1)}, u32[]{:S(2)}, u32[]{:S(2)}) %collective-permute-start.4) | collective-permute-done | bytes 524320 | tf_op jit(solution)/shard_map/cond/branch_1_fun/cond/branch_1_fun/ppermute | solution.py:492
  62.0 1.9 %collective-permute-start.5 = (bf16[2,256,1024]{2,1,0:T(8,128)(2,1)}, bf16[2,256,1024]{2,1,0:T(8,128)(2,1)}, u32[]{:S(2)}, u32[]{:S(2)}) collective-permute-start(bf16[2,256,1024]{2,1,0:T(8,128)(2,1)} %get-tuple-element.87), channel_id=1, source_target_pairs={{7,8},{8,7},{15,16},{16,15},{23,24},{24,23}} | collective-permute-start | bytes 3145736 | tf_op jit(solution)/shard_map/cond/branch_1_fun/cond/branch_1_fun/ppermute | solution.py:495
  64.0 1.0 %join_pieces.3 = bf16[2,256,1024]{2,1,0:T(8,128)(2,1)} custom-call(bf16[2,128,1024]{2,1,0:T(8,128)(2,1)S(1)} %join_pieces.2.first, bf16[2,128,1024]{2,1,0:T(8,128)(2,1)S(1)} %collective-permute-done.4.second), custom_call_target="tpu_custom_call" | custom-call | flops 20000000000 | bytes 20000000000 | tf_op jit(solution)/shard_map/cond/branch_1_fun/cond/branch_1_fun/join_pieces/pallas_call | solution.py:499
  65.0 9.9 %conditional = ((f32[1024,512]{1,0:T(8,128)}, f32[16,512]{1,0:T(8,128)})) conditional(s32[]{:T(128)} %convert_element_type.1, () %tuple.32, (bf16[2,256,1024]{2,1,0:T(8,128)(2,1)}, s32[4,9]{1,0:T(4,128)S(1)}, bf16[512,1024]{1,0:T(8,128)(2,1)}, f32[1024,512]{1,0:T(8,128)}, f32[16,512]{1,0:T(8,128)S(1)}) %tuple.34), branch_computations={%region_8.0_spmd, %region_9.0_spmd} | conditional | flops 1 | bytes 4194353 | solution.py:426
  65.0 2.9 %collective-permute-done.2.rest_1_ = bf16[2,256,1024]{2,1,0:T(8,128)(2,1)S(1)} collective-permute-done((bf16[2,256,1024]{2,1,0:T(8,128)(2,1)}, bf16[2,256,1024]{2,1,0:T(8,128)(2,1)S(1)}, u32[]{:S(2)}, u32[]{:S(2)}) %collective-permute-start.2) | collective-permute-done | bytes 1048608 | tf_op jit(solution)/shard_map/cond/branch_1_fun/cond/branch_1_fun/cond/branch_1_fun/ppermute | solution.py:506
  67.9 7.0 %attend_global.1 = (f32[1024,512]{1,0:T(8,128)}, f32[16,512]{1,0:T(8,128)}) custom-call(s32[4,9]{1,0:T(4,128)S(1)} %get-tuple-element.72.lists_ref, bf16[512,1024]{1,0:T(8,128)(2,1)} %get-tuple-element.73.qs_ref, f32[1024,512]{1,0:T(8,128)} %get-tuple-element.74.acc_ref, f32[16,512]{1,0:T(8,128)S(1)} %get-tuple-element.75.ml_ref, ...), custom_call_target="tpu_custom_call" | custom-call | flops 1 | bytes 1 | tf_op jit(solution)/shard_map/cond/branch_1_fun/cond/branch_1_fun/cond/branch_1_fun/attend_global/pallas_call | solution.py:507
  74.9 7.2 %collective-permute-done.5 = bf16[2,256,1024]{2,1,0:T(8,128)(2,1)} collective-permute-done((bf16[2,256,1024]{2,1,0:T(8,128)(2,1)}, bf16[2,256,1024]{2,1,0:T(8,128)(2,1)}, u32[]{:S(2)}, u32[]{:S(2)}) %collective-permute-start.5) | collective-permute-done | bytes 1048608 | tf_op jit(solution)/shard_map/cond/branch_1_fun/cond/branch_1_fun/ppermute | solution.py:495
  82.1 7.6 %attend_last.1 = bf16[512,1024]{1,0:T(8,128)(2,1)} custom-call(s32[4,9]{1,0:T(4,128)S(1)} %copy-done, bf16[512,512]{1,0:T(8,128)(2,1)} %get-tuple-element.129.place_ref, bf16[512,1024]{1,0:T(8,128)(2,1)} %get-tuple-element.130.qs_ref, f32[1024,512]{1,0:T(8,128)} %get-tuple-element.144.acc_ref, f32[16,512]{1,0:T(8,128)} %get-tuple-element.145.ml_ref, ...), custom_call_target="tpu_custom_call" | custom-call | tf_op jit(solution)/shard_map/attend_last/pallas_call | solution.py:534
  (17 shorter events, 0.9 us)
Async XLA Ops:
  0.0 6.0 %copy-start = (s32[4,9]{1,0:T(4,128)S(1)}, s32[4,9]{1,0:T(4,128)}, u32[]{:S(2)}) copy-start(s32[4,9]{1,0:T(4,128)} %lists_ref.5) | copy-start | bytes 436
  4.6 2.6 %collective-permute-start.9 = (bf16[2,64,1024]{2,1,0:T(8,128)(2,1)S(1)}, bf16[2,64,1024]{2,1,0:T(8,128)(2,1)S(1)}, u32[]{:S(2)}, u32[]{:S(2)}) collective-permute-start(bf16[2,64,1024]{2,1,0:T(8,128)(2,1)S(1)} %get-tuple-element.127), channel_id=1, source_target_pairs={{0,4},{4,0},{8,12},{12,8},{16,20},{20,16},{24,28},{28,24},{1,5},{5... | collective-permute-start | bytes 786440 | tf_op jit(solution)/shard_map/ppermute | solution.py:521
  4.7 28.1 %collective-permute-start.10 = (bf16[2,256,1024]{2,1,0:T(8,128)(2,1)}, bf16[2,256,1024]{2,1,0:T(8,128)(2,1)}, u32[]{:S(2)}, u32[]{:S(2)}) collective-permute-start(bf16[2,256,1024]{2,1,0:T(8,128)(2,1)} %get-tuple-element.137), channel_id=1, source_target_pairs={{1,0},{2,3},{5,6},{6,5},{9,8},{10,11},{13,14},{14,13},{17,16},{18,... | collective-permute-start | bytes 3145736 | tf_op jit(solution)/shard_map/ppermute | solution.py:517
  7.2 0.7 copy-start.1
  7.2 1.2 %copy-start.2 = (bf16[512,1024]{1,0:T(8,128)(2,1)S(1)}, bf16[512,1024]{1,0:T(8,128)(2,1)}, u32[]{:S(2)}) copy-start(bf16[512,1024]{1,0:T(8,128)(2,1)} %param.15) | copy-start | bytes 3145732
  8.5 11.6 %collective-permute-start = (bf16[2,64,1024]{2,1,0:T(8,128)(2,1)S(1)}, bf16[2,64,1024]{2,1,0:T(8,128)(2,1)}, u32[]{:S(2)}, u32[]{:S(2)}) collective-permute-start(bf16[2,64,1024]{2,1,0:T(8,128)(2,1)S(1)} %get-tuple-element.166), channel_id=1, source_target_pairs={{0,1},{3,2},{4,5},{7,6},{8,9},{11,10},{12,13},{15,14},{16,17},{19,... | collective-permute-start | bytes 786440 | tf_op jit(solution)/shard_map/cond/branch_1_fun/ppermute | solution.py:431
  20.1 62.0 %collective-permute-start.11 = (bf16[2,256,1024]{2,1,0:T(8,128)(2,1)S(1)}, bf16[2,256,1024]{2,1,0:T(8,128)(2,1)S(1)}, u32[]{:S(2)}, u32[]{:S(2)}) collective-permute-start(bf16[2,256,1024]{2,1,0:T(8,128)(2,1)S(1)} %get-tuple-element.146), channel_id=1, source_target_pairs={{0,1},{3,2},{4,5},{7,6},{8,9},{11,10},{12,13},{15,14},{16,17},{19,... | collective-permute-start | bytes 3145736 | tf_op jit(solution)/shard_map/ppermute | solution.py:529
  25.6 6.6 %collective-permute-start.1 = (bf16[2,64,1024]{2,1,0:T(8,128)(2,1)S(1)}, bf16[2,64,1024]{2,1,0:T(8,128)(2,1)S(1)}, u32[]{:S(2)}, u32[]{:S(2)}) collective-permute-start(bf16[2,64,1024]{2,1,0:T(8,128)(2,1)S(1)} %get-tuple-element.67.held_ref), channel_id=1, source_target_pairs={{1,2},{2,1},{5,6},{6,5},{9,10},{10,9},{13,14},{14,13},{17,18},{18,... | collective-permute-start | bytes 786440 | tf_op jit(solution)/shard_map/cond/branch_1_fun/ppermute | solution.py:431
  32.8 11.1 %collective-permute-start.6 = (bf16[2,64,1024]{2,1,0:T(8,128)(2,1)S(1)}, bf16[2,64,1024]{2,1,0:T(8,128)(2,1)S(1)}, u32[]{:S(2)}, u32[]{:S(2)}) collective-permute-start(bf16[2,64,1024]{2,1,0:T(8,128)(2,1)S(1)} %get-tuple-element.90.held_ref), channel_id=1, source_target_pairs={{2,3},{1,0},{6,7},{5,4},{10,11},{9,8},{14,15},{13,12},{18,19},{17,... | collective-permute-start | bytes 786440 | tf_op jit(solution)/shard_map/cond/branch_1_fun/ppermute | solution.py:431
  34.1 47.9 %collective-permute-start.7 = (bf16[2,256,1024]{2,1,0:T(8,128)(2,1)}, bf16[2,256,1024]{2,1,0:T(8,128)(2,1)}, u32[]{:S(2)}, u32[]{:S(2)}) collective-permute-start(bf16[2,256,1024]{2,1,0:T(8,128)(2,1)} %get-tuple-element.102), channel_id=1, source_target_pairs={{1,2},{2,1},{5,4},{6,7},{9,10},{10,9},{13,12},{14,15},{17,18},{18,... | collective-permute-start | bytes 3145736 | tf_op jit(solution)/shard_map/cond/branch_1_fun/ppermute | solution.py:471
  44.0 38.1 %collective-permute-start.8 = (bf16[2,256,1024]{2,1,0:T(8,128)(2,1)}, bf16[2,256,1024]{2,1,0:T(8,128)(2,1)}, u32[]{:S(2)}, u32[]{:S(2)}) collective-permute-start(bf16[2,256,1024]{2,1,0:T(8,128)(2,1)} %get-tuple-element.93), channel_id=1, source_target_pairs={{3,4},{4,3},{11,12},{12,11},{19,20},{20,19},{27,28},{28,27}} | collective-permute-start | bytes 3145736 | tf_op jit(solution)/shard_map/cond/branch_1_fun/ppermute | solution.py:483
  46.3 6.4 %collective-permute-start.3 = (bf16[2,64,1024]{2,1,0:T(8,128)(2,1)S(1)}, bf16[2,64,1024]{2,1,0:T(8,128)(2,1)S(1)}, u32[]{:S(2)}, u32[]{:S(2)}) collective-permute-start(bf16[2,64,1024]{2,1,0:T(8,128)(2,1)S(1)} %get-tuple-element.78.first), channel_id=1, source_target_pairs={{0,8},{4,20},{8,0},{12,28},{16,24},{20,4},{24,16},{28,12},{1,9},{5... | collective-permute-start | bytes 786440 | tf_op jit(solution)/shard_map/cond/branch_1_fun/cond/branch_1_fun/ppermute | solution.py:492
  52.8 9.2 %collective-permute-start.4 = (bf16[2,128,1024]{2,1,0:T(8,128)(2,1)S(1)}, bf16[2,128,1024]{2,1,0:T(8,128)(2,1)S(1)}, u32[]{:S(2)}, u32[]{:S(2)}) collective-permute-start(bf16[2,128,1024]{2,1,0:T(8,128)(2,1)S(1)} %join_pieces.2.first), channel_id=1, source_target_pairs={{0,16},{4,12},{8,24},{12,4},{16,0},{20,28},{24,8},{28,20},{1,17},{... | collective-permute-start | bytes 1572872 | tf_op jit(solution)/shard_map/cond/branch_1_fun/cond/branch_1_fun/ppermute | solution.py:492
  62.0 20.0 %collective-permute-start.5 = (bf16[2,256,1024]{2,1,0:T(8,128)(2,1)}, bf16[2,256,1024]{2,1,0:T(8,128)(2,1)}, u32[]{:S(2)}, u32[]{:S(2)}) collective-permute-start(bf16[2,256,1024]{2,1,0:T(8,128)(2,1)} %get-tuple-element.87), channel_id=1, source_target_pairs={{7,8},{8,7},{15,16},{16,15},{23,24},{24,23}} | collective-permute-start | bytes 3145736 | tf_op jit(solution)/shard_map/cond/branch_1_fun/cond/branch_1_fun/ppermute | solution.py:495
  65.0 2.9 %collective-permute-start.2 = (bf16[2,256,1024]{2,1,0:T(8,128)(2,1)}, bf16[2,256,1024]{2,1,0:T(8,128)(2,1)S(1)}, u32[]{:S(2)}, u32[]{:S(2)}) collective-permute-start(bf16[2,256,1024]{2,1,0:T(8,128)(2,1)} %get-tuple-element.76.rest_0_), channel_id=1, source_target_pairs={{0,4},{4,0},{8,12},{12,8},{16,20},{20,16},{24,28},{28,24},{1,5},{5... | collective-permute-start | bytes 3145736 | tf_op jit(solution)/shard_map/cond/branch_1_fun/cond/branch_1_fun/cond/branch_1_fun/ppermute | solution.py:506

commit v3 on v2

--- a/solution.py
+++ b/solution.py
@@ -15,7 +15,7 @@
 HALO = BAND * TILE_POINTS
 PAIR_HEADS = 4
 PAIR = PAIR_HEADS * HEAD_WIDTH
-STATE_ROWS = 8
+STATE_ROWS = 2 * PAIR_HEADS
 MASKED = -1e30
 EXP_SCALE = HEAD_WIDTH ** (-0.5) * 1.4426950408889634
 VMEM_LIMIT = 16 * 1024 * 1024
@@ -51,19 +51,23 @@
     return jnp.bitwise_and(order_ref[...], order_ref.shape[1] - 1)
 
 
-def add_bias(scores, lists_ref, first_query, first_key):
-    parts = []
-    for at in range(scores.shape[0] // TILE_POINTS):
+def bias_rows(lists_ref, queries, keys, first_query, first_key):
+    rows = []
+    for at in range(keys // TILE_POINTS):
         bias = []
-        for query in range(scores.shape[1] // TILE_POINTS):
+        for query in range(queries // TILE_POINTS):
             slot = first_key + at - first_query - query + BAND
             listed = lists_ref[first_query + query, jnp.clip(slot, 0, 2 * BAND)] >= 0
             admitted = listed & (slot >= 0) & (slot <= 2 * BAND)
             value = jnp.where(admitted, 0.0, MASKED).astype(jnp.float32)
             bias.append(jnp.full((1, TILE_POINTS), value, jnp.float32))
-        rows = scores[at * TILE_POINTS : (at + 1) * TILE_POINTS]
-        parts.append(rows + jnp.concatenate(bias, axis=1))
-    return jnp.concatenate(parts, axis=0)
+        rows.append(jnp.concatenate(bias, axis=1))
+    return rows
+
+
+def add_bias(scores, rows):
+    tiles = [scores[at * TILE_POINTS : (at + 1) * TILE_POINTS] + row for at, row in enumerate(rows)]
+    return jnp.concatenate(tiles, axis=0)
 
 
 def exp_of(scores, peak):
@@ -84,6 +88,15 @@
 
 def in_lower_half():
     return lax.axis_index("grp") < lax.axis_size("grp") // 2
+
+
+def at_middle():
+    here, middle = lax.axis_index("grp"), lax.axis_size("grp") // 2
+    return (here == middle) | (here == middle - 1)
+
+
+def meets_early():
+    return in_lower_half() == (lax.rem(lax.axis_index("blk"), 2) == 1)
 
 
 def sort_kernel(lists_hbm, order_hbm, k_hbm, v_hbm, kv_hbm, outward, inward, first_out, second_out, *rest):
@@ -109,13 +122,12 @@
     mine = lax.rem(lax.axis_index("blk"), len(pieces))
     piece_rows = TILE_POINTS // len(pieces)
     low, high = 0, count - HALO
-    outward_first = lax.rem(lax.axis_index("blk"), 2) == 0
     out_start = jnp.where(in_lower_half(), low, high)
     in_start = jnp.where(in_lower_half(), high, low)
-    out_rows = pl.ds(pl.multiple_of(out_start, HALO), HALO)
-    in_rows = pl.ds(pl.multiple_of(in_start, HALO), HALO)
-    first_rows = pl.ds(pl.multiple_of(jnp.where(outward_first, out_start, in_start), HALO), HALO)
-    second_rows = pl.ds(pl.multiple_of(jnp.where(outward_first, in_start, out_start), HALO), HALO)
+    first_start = jnp.where(at_middle() & jnp.logical_not(meets_early()), in_start, out_start)
+    second_start = jnp.where(at_middle() & meets_early(), in_start, out_start)
+    starts = (out_start, in_start, first_start, second_start)
+    out_rows, in_rows, first_rows, second_rows = [pl.ds(pl.multiple_of(start, HALO), HALO) for start in starts]
     leaving = []
     for which in range(2):
         for copy in copies[which * len(copies) // 2 : (which + 1) * len(copies) // 2]:
@@ -148,25 +160,28 @@
     out_ref[...] = jnp.where(rule(lists_ref[0, 2 * BAND + 1]), got_ref[...], held_ref[...])
 
 
-def query_kernel(order_ref, q_ref, qs_ref, place_ref, pick):
+def place_kernel(order_ref, place_ref):
+    place_ref[...] = place_rows(local_order(order_ref))
+
+
+def query_kernel(order_ref, q_ref, qs_ref, pick):
     @pl.when(pl.program_id(0) == 0)
     def _():
-        order = local_order(order_ref)
-        place_ref[...] = place_rows(order)
-        pick[...] = pick_rows(order)
+        pick[...] = pick_rows(local_order(order_ref))
 
     qs_ref[...] = mm(pick[...], q_ref[...]).astype(jnp.bfloat16)
 
 
 def own_kernel(lists_ref, qs_ref, kv_ref, acc_ref, ml_ref):
-    for at in range(PAIR_HEADS):
-        cols = columns_of(at)
-        scores = add_bias(mm_nt(kv_ref[0, :, cols], qs_ref[:, cols]), lists_ref, 0, 0)
-        peak = peak_of(scores)
-        weights = exp_of(scores, peak)
-        ml_ref[at : at + 1] = peak
-        ml_ref[PAIR_HEADS + at : PAIR_HEADS + at + 1] = total_of(weights)
-        acc_ref[cols] = mm_tn(kv_ref[1, :, cols], weights.astype(jnp.bfloat16))
+    count = qs_ref.shape[0]
+    rows = bias_rows(lists_ref, count, count, 0, 0)
+    heads = [columns_of(at) for at in range(PAIR_HEADS)]
+    scores = [add_bias(mm_nt(kv_ref[0, :, cols], qs_ref[:, cols]), rows) for cols in heads]
+    peaks = [peak_of(each) for each in scores]
+    weights = [exp_of(each, peak) for each, peak in zip(scores, peaks)]
+    ml_ref[...] = jnp.concatenate(peaks + [total_of(each) for each in weights], axis=0)
+    for cols, each in zip(heads, weights):
+        acc_ref[cols] = mm_tn(kv_ref[1, :, cols], each.astype(jnp.bfloat16))
 
 
 def halo_place(is_low, count):
@@ -175,22 +190,14 @@
     return start, jnp.where(is_low, 0, tiles - BAND), jnp.where(is_low, -BAND, tiles)
 
 
-def take_keys(old, scores, values, summed):
-    old_peak, old_total = old
-    peak = jnp.maximum(old_peak, peak_of(scores))
-    shrink = exp_of(old_peak, peak)
-    weights = exp_of(scores, peak)
-    total = old_total * shrink + total_of(weights)
-    return peak, total, summed * shrink + mm_tn(values, weights.astype(jnp.bfloat16))
-
-
-def at_middle():
-    here, middle = lax.axis_index("grp"), lax.axis_size("grp") // 2
-    return (here == middle) | (here == middle - 1)
-
-
-def meets_early():
-    return at_middle() == (lax.rem(lax.axis_index("blk"), 2) == 1)
+def take_keys(ml, scores, values, summed):
+    old = [ml[at : at + 1] for at in range(2 * PAIR_HEADS)]
+    peaks = [jnp.maximum(was, peak_of(each)) for was, each in zip(old, scores)]
+    weights = [exp_of(each, peak) for each, peak in zip(scores, peaks)]
+    shrinks = [exp_of(was, peak) for was, peak in zip(old, peaks)]
+    products = [mm_tn(value, each.astype(jnp.bfloat16)) for value, each in zip(values, weights)]
+    totals = [was * shrink + total_of(each) for was, shrink, each in zip(old[PAIR_HEADS:], shrinks, weights)]
+    return peaks, totals, [was * shrink + new for was, shrink, new in zip(summed, shrinks, products)]
 
 
 def near_kernel(lists_ref, qs_ref, near_kv, acc_ref, ml_ref, new_acc_ref, new_ml_ref):
@@ -201,78 +208,92 @@
     def _():
         start, first_query, first_key = halo_place(jnp.logical_not(in_lower_half()), qs_ref.shape[0])
         met = pl.ds(start, HALO)
-        for at in range(PAIR_HEADS):
-            cols = columns_of(at)
-            scores = mm_nt(near_kv[0, :, cols], qs_ref[met, cols])
-            scores = add_bias(scores, lists_ref, first_query, first_key)
-            old = ml_ref[at : at + 1, met], ml_ref[PAIR_HEADS + at : PAIR_HEADS + at + 1, met]
-            peak, total, summed = take_keys(old, scores, near_kv[1, :, cols], acc_ref[cols, met])
-            new_acc_ref[cols, met] = summed
-            new_ml_ref[at : at + 1, met] = peak
-            new_ml_ref[PAIR_HEADS + at : PAIR_HEADS + at + 1, met] = total
+        rows = bias_rows(lists_ref, HALO, HALO, first_query, first_key)
+        heads = [columns_of(at) for at in range(PAIR_HEADS)]
+        scores = [add_bias(mm_nt(near_kv[0, :, cols], qs_ref[met, cols]), rows) for cols in heads]
+        values = [near_kv[1, :, cols] for cols in heads]
+        summed = [acc_ref[cols, met] for cols in heads]
+        peaks, totals, summed = take_keys(ml_ref[:, met], scores, values, summed)
+        for cols, each in zip(heads, summed):
+            new_acc_ref[cols, met] = each
+        new_ml_ref[:, met] = jnp.concatenate(peaks + totals, axis=0)
 
 
 def global_kernel(lists_ref, qs_ref, acc_ref, ml_ref, *rest):
     pieces, (new_acc_ref, new_ml_ref) = rest[:-2], rest[-2:]
-    for at in range(PAIR_HEADS):
-        cols = columns_of(at)
-        old = ml_ref[at : at + 1], ml_ref[PAIR_HEADS + at : PAIR_HEADS + at + 1]
-        keys = jnp.concatenate([ref[0, :, cols] for ref in pieces], axis=0)
-        values = jnp.concatenate([ref[1, :, cols] for ref in pieces], axis=0)
-        peak, total, summed = take_keys(old, mm_nt(keys, qs_ref[:, cols]), values, acc_ref[cols])
-        new_acc_ref[cols] = summed
-        new_ml_ref[at : at + 1] = peak
-        new_ml_ref[PAIR_HEADS + at : PAIR_HEADS + at + 1] = total
+    heads = [columns_of(at) for at in range(PAIR_HEADS)]
+    keys = [jnp.concatenate([ref[0, :, cols] for ref in pieces], axis=0) for cols in heads]
+    values = [jnp.concatenate([ref[1, :, cols] for ref in pieces], axis=0) for cols in heads]
+    scores = [mm_nt(each, qs_ref[:, cols]) for each, cols in zip(keys, heads)]
+    summed = [acc_ref[cols] for cols in heads]
+    peaks, totals, summed = take_keys(ml_ref[...], scores, values, summed)
+    for cols, each in zip(heads, summed):
+        new_acc_ref[cols] = each
+    new_ml_ref[...] = jnp.concatenate(peaks + totals, axis=0)
 
 
 def finish_kernel(lists_ref, place_ref, qs_ref, acc_ref, ml_ref, *rest):
-    next_kv, late_kv, even_kv, odd_kv, out_ref, attended, halos, arrived = rest
+    next_kv, second_kv, odd_kv, out_ref, attended, halos, arrived = rest
     count = qs_ref.shape[0]
     here, end = lax.axis_index("grp"), lax.axis_size("grp") - 1
     at_end = (here == 0) | (here == end)
     even_wrap = (lax.rem(lax.axis_index("blk"), 2) == 0) == (here == end)
     sources = (
         (jnp.logical_not(at_end), 0, next_kv),
-        (at_end & even_wrap, 0, even_kv),
+        (at_end & even_wrap, 0, second_kv),
         (at_end & jnp.logical_not(even_wrap), 0, odd_kv),
-        (jnp.logical_not(meets_early()), 1, late_kv),
+        (jnp.logical_not(meets_early()), 1, second_kv),
     )
     step = pl.program_id(0)
 
+    blocks = halos.shape[3] // PAIR
+
+    def copies_of(side, source, block):
+        cols = pl.ds(block * PAIR, PAIR)
+        return [
+            pltpu.make_async_copy(source.at[w, :, cols], halos.at[side, w, :, cols], arrived.at[side, w, block])
+            for w in range(2)
+        ]
+
     @pl.when(step == 0)
     def _():
-        copies = []
-        for chosen, side, source in sources:
-            pieces = [
-                pltpu.make_async_copy(source.at[w], halos.at[side, w], arrived.at[side, w]) for w in range(2)
-            ]
-            copies.append((chosen, pieces))
-
-            @pl.when(chosen)
-            def _():
-                for copy in pieces:
-                    copy.start()
-
-        for chosen, pieces in copies:
-
-            @pl.when(chosen)
-            def _():
-                for copy in pieces:
-                    copy.wait()
+        for block in range(blocks):
+            for chosen, side, source in sources:
+
+                @pl.when(chosen)
+                def _():
+                    for copy in copies_of(side, source, block):
+                        copy.start()
+
+    def wait_for(side):
+        for block in range(blocks):
+            for chosen, here_side, source in sources:
+                if here_side == side:
+
+                    @pl.when(chosen & (step == block))
+                    def _():
+                        for copy in copies_of(side, source, block):
+                            copy.wait()
 
     def add_halo(side, is_low):
         start, first_query, first_key = halo_place(is_low, count)
         met = pl.ds(start, HALO)
-        for at in range(PAIR_HEADS):
-            cols = columns_of(at)
-            here_cols = pl.ds(pl.multiple_of(step * PAIR + at * HEAD_WIDTH, HEAD_WIDTH), HEAD_WIDTH)
-            scores = mm_nt(halos[side, 0, :, here_cols], qs_ref[met, cols])
-            scores = add_bias(scores, lists_ref, first_query, first_key)
-            old = ml_ref[at : at + 1, met], ml_ref[PAIR_HEADS + at : PAIR_HEADS + at + 1, met]
-            _, total, summed = take_keys(old, scores, halos[side, 1, :, here_cols], acc_ref[cols, met])
-            attended[cols, met] = (summed / total).astype(jnp.bfloat16)
-
+        rows = bias_rows(lists_ref, HALO, HALO, first_query, first_key)
+        heads = [columns_of(at) for at in range(PAIR_HEADS)]
+        here_cols = [
+            pl.ds(pl.multiple_of(step * PAIR + at * HEAD_WIDTH, HEAD_WIDTH), HEAD_WIDTH) for at in range(PAIR_HEADS)
+        ]
+        keys = [halos[side, 0, :, cols] for cols in here_cols]
+        values = [halos[side, 1, :, cols] for cols in here_cols]
+        scores = [add_bias(mm_nt(key, qs_ref[met, cols]), rows) for key, cols in zip(keys, heads)]
+        summed = [acc_ref[cols, met] for cols in heads]
+        _, totals, summed = take_keys(ml_ref[:, met], scores, values, summed)
+        for cols, each, total in zip(heads, summed, totals):
+            attended[cols, met] = (each / total).astype(jnp.bfloat16)
+
+    wait_for(0)
     add_halo(0, in_lower_half())
+    wait_for(1)
 
     @pl.when(jnp.logical_not(meets_early()))
     def _():
@@ -407,9 +428,9 @@
     def exchange(turn):
         links = []
         for run in range(blk_count):
-            chosen = (away, across)[(run + turn) % 2]
-            links += [(run * grp_count + i, run * grp_count + j) for i, j in chosen]
-        return links
+            down = (run + turn) % 2 == 1
+            links += [(run * grp_count + i, run * grp_count + j) for i, j in away + across if (j < i) == down]
+        return links + wraps[0] if turn == 1 else links
 
     wraps = [[], []]
     for run in range(1, blk_count):
@@ -425,10 +446,10 @@
         skip = lambda *_: jax.tree.map(lambda leaf: jnp.zeros(leaf.shape, leaf.dtype), shapes)
         return lax.cond(listed, run, skip, *operands)
 
-    def send(piece, some):
-        for pairs, rule in some[:-1]:
+    def relay(piece, some):
+        for pairs, rule in some:
             piece = take(rule, lax.ppermute(piece, "grp", pairs), piece)
-        return piece, lax.ppermute(piece, "grp", some[-1][0])
+        return piece
 
     def take(rule, got, piece, **cost):
         return select(lambda tile_id: rule(owner_of(tile_id)[1]), got, piece, **cost)
@@ -442,17 +463,17 @@
     inward_rounds, across_round, outward_rounds = rounds[:inner], rounds[inner], rounds[inner + 1 :]
 
     def inward_stage(piece):
-        queries, place = call(
+        queries = call(
             query_kernel,
             "sort_queries",
             [whole_block(1, row_count), queries_block],
-            [queries_block, whole_block(row_count, row_count)],
-            [bf16((row_count, feature_count)), bf16((row_count, row_count))],
+            queries_block,
+            bf16((row_count, feature_count)),
             [pltpu.VMEM((row_count, row_count), jnp.bfloat16)],
             cost=busy,
             grid=grid,
         )(order, query_rows)
-        return *send(piece, inward_rounds), queries, place
+        return lax.ppermute(piece, "grp", inward_rounds[-1][0]), queries
 
     def across_stage(piece, kv, queries):
         own = call(
@@ -464,11 +485,14 @@
             cost=busy,
             grid=grid,
         )(tile_lists, queries, kv)
-        piece, got = send(piece, [across_round])
-        return take(across_round[1], got, piece), own
+        return relay(piece, [across_round]), own
 
     def outward_stage(piece, outward, second_out, queries, own, near_kv):
-        late_kv = lax.ppermute(second_out, ("blk", "grp"), exchange(1))
+        place = call(
+            place_kernel, "place_rows", [VMEM], VMEM, bf16((row_count, row_count)), cost=busy
+        )(order)
+        place, second_out = tie((place, second_out))
+        second_kv = lax.ppermute(second_out, ("blk", "grp"), exchange(1))
         own = call(
             near_kernel,
             "attend_near",
@@ -478,12 +502,11 @@
             cost=busy,
             grid=grid,
         )(tile_lists, queries, near_kv, *own)
-        piece, got = send(piece, outward_rounds)
-        got, outward = tie((got, outward))
-        even_kv = lax.ppermute(outward, ("blk", "grp"), wraps[0])
+        piece = relay(piece, outward_rounds[:-1])
+        got = lax.ppermute(piece, "grp", outward_rounds[-1][0])
         piece = take(outward_rounds[-1][1], got, piece, flops=LONG)
         states, odd_kv = stage(plane_stage, piece, outward, queries, own)
-        return states, late_kv, even_kv, odd_kv
+        return states, place, second_kv, odd_kv
 
     def plane_stage(piece, outward, queries, own):
         for step in range(2):
@@ -524,26 +547,27 @@
             return lax.rem(lax.axis_index("blk") + part - step, part) == owner_of(tile_id)[0]
 
         piece = select(from_owner, got, piece, flops=LONG)
-    piece, got, queries, place = stage(inward_stage, piece)
+    piece = relay(piece, inward_rounds[:-1])
+    got, queries = stage(inward_stage, piece)
     got, inward = tie((got, inward))
     next_kv = lax.ppermute(inward, "grp", towards)
     piece = take(inward_rounds[-1][1], got, piece)
     piece, own = stage(across_stage, piece, kv, queries)
     piece, near_kv = tie((piece, near_kv))
-    states, late_kv, even_kv, odd_kv = stage(outward_stage, piece, outward, second_out, queries, own, near_kv)
+    states, place, second_kv, odd_kv = stage(outward_stage, piece, outward, second_out, queries, own, near_kv)
     return call(
         finish_kernel,
         "attend_last",
-        [SMEM, whole_block(row_count, row_count), queries_block] + state_blocks + [ANY] * 4,
+        [SMEM, whole_block(row_count, row_count), queries_block] + state_blocks + [ANY] * 3,
         queries_block,
         bf16((row_count, feature_count)),
         [
             pltpu.VMEM((PAIR, row_count), jnp.bfloat16),
             pltpu.VMEM((2, 2, HALO, feature_count), jnp.bfloat16),
-            pltpu.SemaphoreType.DMA((2, 2)),
+            pltpu.SemaphoreType.DMA((2, 2, grid[0])),
         ],
         grid=grid,
-    )(tile_lists, place, queries, *states, next_kv, late_kv, even_kv, odd_kv)
+    )(tile_lists, place, queries, *states, next_kv, second_kv, odd_kv)
 
 
 def solution(mesh):

time: 90.1 us -> 85.3 us (0.947)
  Pallas kernels: 36.1 us -> 32.1 us
  waiting for transfers between devices: 30.4 us -> 28.4 us
  starting transfers between devices: 21.2 us -> 22.3 us
    pallas_call x1, Pallas kernels: 4.9 us -> 2.63 us  [outward_stage(): call(near_kernel, 'attend_near', [SMEM, queries_block, column_block(2, HA...]
    ppermute x1, starting transfers between devices: 1.91 us -> 3.67 us  [plane_stage(): odd_kv = lax.ppermute(outward, ('blk', 'grp'), wraps[1])]
    ppermute x5 -> x4, starting transfers between devices: 11.7 us -> 10.3 us  [the longest x1 7.02 us: inward_stage(): return (lax.ppermute(piece, 'grp', inward_rounds[-1][0]), queries)]
    pallas_call x1, Pallas kernels: 7 us -> 5.68 us  [global_stage(): call(global_kernel, 'attend_global', [SMEM, queries_block] + state_blocks...]
    ppermute x5 -> x4, waiting for transfers between devices: 6.37 us -> 5.24 us  [the longest x1 4.05 us: outward_stage(): got = lax.ppermute(piece, 'grp', outward_rounds[-1][0])]
    pallas_call x1, Pallas kernels: 5.87 us -> 4.8 us  [across_stage(): call(own_kernel, 'attend_own', [SMEM, queries_block, column_block(2, row_...]
    pallas_call x0 -> x1, Pallas kernels: none -> 0.9 us  [outward_stage(): call(place_kernel, 'place_rows', [VMEM], VMEM, bf16((row_count, row_count...]
  transfers between devices with their start and end apart: 12 -> 11, of which waited for: 6 -> 6; matrix products, arithmetic and copies ran while one was open for 1% -> 1% of each run, Pallas kernels for 27% -> 23%
where the time goes in v3:
time: 85.3 us; the launch traced here: 84.9 us
  Pallas kernels  32.1 us (38%)
  waiting for transfers between devices  28.4 us (33%)
  starting transfers between devices  22.3 us (26%)
  local copies, waits for them, and re-layouts  1.21 us (1%)
    ppermute x2, waiting for transfers between devices, plane_stage(): got = lax.ppermute(piece, 'blk', links)  13.5 us
    pallas_call x1, Pallas kernels, body(): call(finish_kernel, 'attend_last', [SMEM, whole_block(row_count, row_coun...  7.62 us
    ppermute x1, starting transfers between devices, inward_stage(): return (lax.ppermute(piece, 'grp', inward_rounds[-1][0]), queries)  7.02 us
    ppermute x1, waiting for transfers between devices, plane_stage(): odd_kv = lax.ppermute(outward, ('blk', 'grp'), wraps[1])  6.76 us
    pallas_call x1, Pallas kernels, global_stage(): call(global_kernel, 'attend_global', [SMEM, queries_block] + state_blocks...  5.68 us
    pallas_call x1, Pallas kernels, across_stage(): call(own_kernel, 'attend_own', [SMEM, queries_block, column_block(2, row_...  4.8 us
    pallas_call x1, Pallas kernels, body(): call(sort_kernel, 'sort_keys_values', [HBM] * 4, [ANY] * (5 + part), [bf1...  4.64 us
    ppermute x1, starting transfers between devices, body(): next_kv = lax.ppermute(inward, 'grp', towards)  4.55 us
  transfers between devices with their start and end apart: 11, of which 6 were waited for; matrix products, arithmetic and copies ran while one was open for 1% of the time, Pallas kernels for 23%

profile of v3, /device:TPU:4, one launch (start us, length us, event | category | flops | bytes accessed | tf_op | source)
XLA Modules:
  0.0 84.9 jit_solution(11307685869998121884)
XLA Ops:
  0.0 4.6 %sort_keys_values.1 = (bf16[2,512,1024]{2,1,0:T(8,128)(2,1)}, bf16[2,256,1024]{2,1,0:T(8,128)(2,1)}, bf16[2,256,1024]{2,1,0:T(8,128)(2,1)S(1)}, bf16[2,256,1024]...) custom-call(s32[4,9]{1,0:T(4,128)} %lists_ref.5, ...), custom_call_target="tpu_custom_call" | custom-call | tf_op jit(solution)/shard_map/sort_keys_values/pallas_call | solution.py:390
  4.7 1.6 %collective-permute-start.9 = (bf16[2,256,1024]{2,1,0:T(8,128)(2,1)}, bf16[2,256,1024]{2,1,0:T(8,128)(2,1)}, u32[]{:S(2)}, u32[]{:S(2)}) collective-permute-start(bf16[2,256,1024]{2,1,0:T(8,128)(2,1)} %get-tuple-element.134), channel_id=1, source_target_pairs={{2,3},{1,2},{5,4},{6,5},{10,11},{9,10},{13,12},{14,13},{18,19},{17... | collective-permute-start | bytes 3145736 | tf_op jit(solution)/shard_map/ppermute | solution.py:540
  6.4 0.6 slice.3
  7.6 0.6 select_piece.6.held_ref
  8.9 10.2 %conditional.5 = (bf16[2,64,1024]{2,1,0:T(8,128)(2,1)}, bf16[512,1024]{1,0:T(8,128)(2,1)}) conditional(s32[]{:T(128)} %convert_element_type.11, () %tuple.50, (bf16[2,64,1024]{2,1,0:T(8,128)(2,1)S(1)}, s32[1,512]{1,0:T(1,128)S(1)}, bf16[512,1024]{1,0:T(8,128)(2,1)S(1)}) %tuple.72), branch_computations={%region_0.0_spmd, %region_1.0_spmd} | conditional | flops 20000000000 | bytes 20001048576 | solution.py:447
  8.9 7.0 %collective-permute-start = (bf16[2,64,1024]{2,1,0:T(8,128)(2,1)S(1)}, bf16[2,64,1024]{2,1,0:T(8,128)(2,1)}, u32[]{:S(2)}, u32[]{:S(2)}) collective-permute-start(bf16[2,64,1024]{2,1,0:T(8,128)(2,1)S(1)} %get-tuple-element.63), channel_id=1, source_target_pairs={{0,1},{3,2},{4,5},{7,6},{8,9},{11,10},{12,13},{15,14},{16,17},{19,... | collective-permute-start | bytes 786440 | tf_op jit(solution)/shard_map/cond/branch_1_fun/ppermute | solution.py:476
  15.9 2.0 %sort_queries.1 = bf16[512,1024]{1,0:T(8,128)(2,1)} custom-call(s32[1,512]{1,0:T(1,128)S(1)} %get-tuple-element.64.order_ref, bf16[512,1024]{1,0:T(8,128)(2,1)S(1)} %get-tuple-element.148.q_ref), custom_call_target="tpu_custom_call" | custom-call | flops 20000000000 | bytes 20000000000 | tf_op jit(solution)/shard_map/cond/branch_1_fun/sort_queries/pallas_call | solution.py:466
  17.9 1.2 %collective-permute-done = bf16[2,64,1024]{2,1,0:T(8,128)(2,1)} collective-permute-done((bf16[2,64,1024]{2,1,0:T(8,128)(2,1)S(1)}, bf16[2,64,1024]{2,1,0:T(8,128)(2,1)}, u32[]{:S(2)}, u32[]{:S(2)}) %collective-permute-start) | collective-permute-done | bytes 262176 | tf_op jit(solution)/shard_map/cond/branch_1_fun/ppermute | solution.py:476
  19.0 4.5 %collective-permute-start.10 = (bf16[2,256,1024]{2,1,0:T(8,128)(2,1)S(1)}, bf16[2,256,1024]{2,1,0:T(8,128)(2,1)S(1)}, u32[]{:S(2)}, u32[]{:S(2)}) collective-permute-start(bf16[2,256,1024]{2,1,0:T(8,128)(2,1)S(1)} %get-tuple-element.144), channel_id=1, source_target_pairs={{0,1},{3,2},{4,5},{7,6},{8,9},{11,10},{12,13},{15,14},{16,17},{19,... | collective-permute-start | bytes 3145736 | tf_op jit(solution)/shard_map/ppermute | solution.py:553
  23.6 1.0 %select_piece.7 = bf16[2,64,1024]{2,1,0:T(8,128)(2,1)S(1)} custom-call(s32[4,9]{1,0:T(4,128)S(1)} %copy-done, bf16[2,64,1024]{2,1,0:T(8,128)(2,1)} %get-tuple-element.130.got_ref, bf16[2,64,1024]{2,1,0:T(8,128)(2,1)S(1)} %select_piece.6.held_ref), custom_call_target="tpu_custom_call" | custom-call | flops 1 | bytes 1 | tf_op jit(solution)/shard_map/select_piece/pallas_call | solution.py:414
  24.6 6.1 %conditional.6 = (bf16[2,64,1024]{2,1,0:T(8,128)(2,1)S(1)}, f32[1024,512]{1,0:T(8,128)S(1)}, f32[16,512]{1,0:T(8,128)S(1)}) conditional(s32[]{:T(128)} %convert_element_type.11, () %tuple.49, (bf16[2,64,1024]{2,1,0:T(8,128)(2,1)S(1)}, s32[4,9]{1,0:T(4,128)S(1)}, bf16[512,1024]{1,0:T(8,128)(2,1)}, bf16[2,512,1024]{2,1,0:T(8,128)(2,1)}) %tuple.68), branch_computations={%region_2.0_spmd, %region_3.0_spmd} | conditional | flops 20000000000 | bytes 20001048576 | solution.py:447
  24.6 0.7 collective-permute-start.1
  25.3 4.8 %attend_own.1 = (f32[1024,512]{1,0:T(8,128)S(1)}, f32[16,512]{1,0:T(8,128)S(1)}) custom-call(s32[4,9]{1,0:T(4,128)S(1)} %get-tuple-element.66.lists_ref, bf16[512,1024]{1,0:T(8,128)(2,1)} %get-tuple-element.68.qs_ref, bf16[2,512,1024]{2,1,0:T(8,128)(2,1)} %get-tuple-element.69.kv_ref), custom_call_target="tpu_custom_call" | custom-call | flops 20000000000 | bytes 20000000000 | tf_op jit(solution)/shard_map/cond/branch_1_fun/attend_own/pallas_call | solution.py:479
  30.1 0.6 select_piece.4
  30.7 46.6 %conditional.7 = (f32[1024,512]{1,0:T(8,128)}, f32[16,512]{1,0:T(8,128)}, bf16[512,512]{1,0:T(8,128)(2,1)}, bf16[2,256,1024]{2,1,0:T(8,128)(2,1)}, bf16[2,256,1024]{2,1,0:T(8,128)(2,1)}) conditional(s32[]{:T(128)} %convert_element_type.11, () %tuple.48, (pred[]{:T(512)}, bf16[2,64,1024]{2,1,0:T(8,128)(2,1)S(1)}, s32[4,9]{1,0:T(4,128)S(1)}, ...), branch_computations={%region_4.0_spmd, %region_5.0_spmd} | conditional | flops 80000000000 | bytes 80016777216 | solution.py:447
  30.8 1.3 %collective-permute-start.6 = (bf16[2,64,1024]{2,1,0:T(8,128)(2,1)S(1)}, bf16[2,64,1024]{2,1,0:T(8,128)(2,1)S(1)}, u32[]{:S(2)}, u32[]{:S(2)}) collective-permute-start(bf16[2,64,1024]{2,1,0:T(8,128)(2,1)S(1)} %get-tuple-element.90.held_ref), channel_id=1, source_target_pairs={{2,3},{1,0},{6,7},{5,4},{10,11},{9,8},{14,15},{13,12},{18,19},{17,... | collective-permute-start | bytes 786440 | tf_op jit(solution)/shard_map/cond/branch_1_fun/ppermute | solution.py:506
  32.1 0.9 %place_rows.1 = bf16[512,512]{1,0:T(8,128)(2,1)} custom-call(s32[1,512]{1,0:T(1,128)S(1)} %get-tuple-element.100.order_ref), custom_call_target="tpu_custom_call" | custom-call | flops 20000000000 | bytes 20000000000 | tf_op jit(solution)/shard_map/cond/branch_1_fun/place_rows/pallas_call | solution.py:491
  33.0 1.3 %collective-permute-start.7 = (bf16[2,256,1024]{2,1,0:T(8,128)(2,1)}, bf16[2,256,1024]{2,1,0:T(8,128)(2,1)}, u32[]{:S(2)}, u32[]{:S(2)}) collective-permute-start(bf16[2,256,1024]{2,1,0:T(8,128)(2,1)} %get-tuple-element.103), channel_id=1, source_target_pairs={{1,0},{2,1},{6,7},{5,6},{9,8},{10,9},{14,15},{13,14},{17,16},{18,1... | collective-permute-start | bytes 3145736 | tf_op jit(solution)/shard_map/cond/branch_1_fun/ppermute | solution.py:495
  34.3 2.6 %attend_near.1 = (f32[1024,512]{1,0:T(8,128)}, f32[16,512]{1,0:T(8,128)S(1)}) custom-call(s32[4,9]{1,0:T(4,128)S(1)} %get-tuple-element.89.lists_ref, bf16[512,1024]{1,0:T(8,128)(2,1)} %get-tuple-element.92.qs_ref, bf16[2,256,1024]{2,1,0:T(8,128)(2,1)} %get-tuple-element.93.near_kv, f32[1024,512]{1,0:T(8,128)S(1)} %get-tuple-element.94.acc_ref, ...), custom_call_target="tpu_custom_call" | custom-call | flops 20000000000 | bytes 20000000000 | tf_op jit(solution)/shard_map/cond/branch_1_fun/attend_near/pallas_call | solution.py:496
  36.9 4.1 %collective-permute-done.6.got_ref = bf16[2,64,1024]{2,1,0:T(8,128)(2,1)S(1)} collective-permute-done((bf16[2,64,1024]{2,1,0:T(8,128)(2,1)S(1)}, bf16[2,64,1024]{2,1,0:T(8,128)(2,1)S(1)}, u32[]{:S(2)}, u32[]{:S(2)}) %collective-permute-start.6) | collective-permute-done | bytes 262176 | tf_op jit(solution)/shard_map/cond/branch_1_fun/ppermute | solution.py:506
  40.9 0.6 select_piece.5
  41.5 35.8 %conditional.1 = (f32[1024,512]{1,0:T(8,128)}, f32[16,512]{1,0:T(8,128)}, bf16[2,256,1024]{2,1,0:T(8,128)(2,1)}) conditional(s32[]{:T(128)} %convert_element_type.2, () %tuple.36, (pred[]{:T(512)}, bf16[2,64,1024]{2,1,0:T(8,128)(2,1)S(1)}, bf16[2,256,1024]{2,1,0:T(8,128)(2,1)}, s32[4,9]{1,0:T(4,128)S(1)}, bf16[512,1024]{1,0:T(8,128)(2,1)}, ...), branch_computations={%region_6.0_spmd, %region_7.0_spmd} | conditional | flops 20000000000 | bytes 20011534336 | solution.py:447
  41.6 1.6 %collective-permute-start.3 = (bf16[2,64,1024]{2,1,0:T(8,128)(2,1)S(1)}, bf16[2,64,1024]{2,1,0:T(8,128)(2,1)S(1)}, u32[]{:S(2)}, u32[]{:S(2)}) collective-permute-start(bf16[2,64,1024]{2,1,0:T(8,128)(2,1)S(1)} %get-tuple-element.78.first), channel_id=1, source_target_pairs={{0,8},{4,20},{8,0},{12,28},{16,24},{20,4},{24,16},{28,12},{1,9},{5... | collective-permute-start | bytes 786440 | tf_op jit(solution)/shard_map/cond/branch_1_fun/cond/branch_1_fun/ppermute | solution.py:515
  43.1 4.9 %collective-permute-done.3.second = bf16[2,64,1024]{2,1,0:T(8,128)(2,1)S(1)} collective-permute-done((bf16[2,64,1024]{2,1,0:T(8,128)(2,1)S(1)}, bf16[2,64,1024]{2,1,0:T(8,128)(2,1)S(1)}, u32[]{:S(2)}, u32[]{:S(2)}) %collective-permute-start.3) | collective-permute-done | bytes 262176 | tf_op jit(solution)/shard_map/cond/branch_1_fun/cond/branch_1_fun/ppermute | solution.py:515
  48.6 8.7 %collective-permute-done.4.second = bf16[2,128,1024]{2,1,0:T(8,128)(2,1)S(1)} collective-permute-done((bf16[2,128,1024]{2,1,0:T(8,128)(2,1)S(1)}, bf16[2,128,1024]{2,1,0:T(8,128)(2,1)S(1)}, u32[]{:S(2)}, u32[]{:S(2)}) %collective-permute-start.4) | collective-permute-done | bytes 524320 | tf_op jit(solution)/shard_map/cond/branch_1_fun/cond/branch_1_fun/ppermute | solution.py:515
  57.3 3.7 %collective-permute-start.5 = (bf16[2,256,1024]{2,1,0:T(8,128)(2,1)}, bf16[2,256,1024]{2,1,0:T(8,128)(2,1)}, u32[]{:S(2)}, u32[]{:S(2)}) collective-permute-start(bf16[2,256,1024]{2,1,0:T(8,128)(2,1)} %get-tuple-element.87), channel_id=1, source_target_pairs={{7,8},{8,7},{15,16},{16,15},{23,24},{24,23}} | collective-permute-start | bytes 3145736 | tf_op jit(solution)/shard_map/cond/branch_1_fun/cond/branch_1_fun/ppermute | solution.py:518
  61.0 1.0 %join_pieces.3 = bf16[2,256,1024]{2,1,0:T(8,128)(2,1)} custom-call(bf16[2,128,1024]{2,1,0:T(8,128)(2,1)S(1)} %join_pieces.2.first, bf16[2,128,1024]{2,1,0:T(8,128)(2,1)S(1)} %collective-permute-done.4.second), custom_call_target="tpu_custom_call" | custom-call | flops 20000000000 | bytes 20000000000 | tf_op jit(solution)/shard_map/cond/branch_1_fun/cond/branch_1_fun/join_pieces/pallas_call | solution.py:522
  62.0 8.6 %conditional = ((f32[1024,512]{1,0:T(8,128)}, f32[16,512]{1,0:T(8,128)})) conditional(s32[]{:T(128)} %convert_element_type.1, () %tuple.32, (bf16[2,256,1024]{2,1,0:T(8,128)(2,1)}, s32[4,9]{1,0:T(4,128)S(1)}, bf16[512,1024]{1,0:T(8,128)(2,1)}, f32[1024,512]{1,0:T(8,128)}, f32[16,512]{1,0:T(8,128)S(1)}) %tuple.34), branch_computations={%region_8.0_spmd, %region_9.0_spmd} | conditional | flops 1 | bytes 4194353 | solution.py:447
  62.0 2.9 %collective-permute-done.2.rest_1_ = bf16[2,256,1024]{2,1,0:T(8,128)(2,1)S(1)} collective-permute-done((bf16[2,256,1024]{2,1,0:T(8,128)(2,1)}, bf16[2,256,1024]{2,1,0:T(8,128)(2,1)S(1)}, u32[]{:S(2)}, u32[]{:S(2)}) %collective-permute-start.2) | collective-permute-done | bytes 1048608 | tf_op jit(solution)/shard_map/cond/branch_1_fun/cond/branch_1_fun/cond/branch_1_fun/ppermute | solution.py:529
  64.9 5.7 %attend_global.1 = (f32[1024,512]{1,0:T(8,128)}, f32[16,512]{1,0:T(8,128)}) custom-call(s32[4,9]{1,0:T(4,128)S(1)} %get-tuple-element.72.lists_ref, bf16[512,1024]{1,0:T(8,128)(2,1)} %get-tuple-element.73.qs_ref, f32[1024,512]{1,0:T(8,128)} %get-tuple-element.74.acc_ref, f32[16,512]{1,0:T(8,128)S(1)} %get-tuple-element.75.ml_ref, ...), custom_call_target="tpu_custom_call" | custom-call | flops 1 | bytes 1 | tf_op jit(solution)/shard_map/cond/branch_1_fun/cond/branch_1_fun/cond/branch_1_fun/attend_global/pallas_call | solution.py:530
  70.6 6.8 %collective-permute-done.5 = bf16[2,256,1024]{2,1,0:T(8,128)(2,1)} collective-permute-done((bf16[2,256,1024]{2,1,0:T(8,128)(2,1)}, bf16[2,256,1024]{2,1,0:T(8,128)(2,1)}, u32[]{:S(2)}, u32[]{:S(2)}) %collective-permute-start.5) | collective-permute-done | bytes 1048608 | tf_op jit(solution)/shard_map/cond/branch_1_fun/cond/branch_1_fun/ppermute | solution.py:518
  77.3 7.6 %attend_last.1 = bf16[512,1024]{1,0:T(8,128)(2,1)} custom-call(s32[4,9]{1,0:T(4,128)S(1)} %copy-done, bf16[512,512]{1,0:T(8,128)(2,1)} %get-tuple-element.141.place_ref, bf16[512,1024]{1,0:T(8,128)(2,1)} %get-tuple-element.131.qs_ref, f32[1024,512]{1,0:T(8,128)} %get-tuple-element.142.acc_ref, f32[16,512]{1,0:T(8,128)} %get-tuple-element.143.ml_ref, ...), custom_call_target="tpu_custom_call" | custom-call | tf_op jit(solution)/shard_map/attend_last/pallas_call | solution.py:558
  (15 shorter events, 1.3 us)
Async XLA Ops:
  0.0 6.4 %copy-start = (s32[4,9]{1,0:T(4,128)S(1)}, s32[4,9]{1,0:T(4,128)}, u32[]{:S(2)}) copy-start(s32[4,9]{1,0:T(4,128)} %lists_ref.5) | copy-start | bytes 436
  4.7 3.0 %collective-permute-start.8 = (bf16[2,64,1024]{2,1,0:T(8,128)(2,1)S(1)}, bf16[2,64,1024]{2,1,0:T(8,128)(2,1)S(1)}, u32[]{:S(2)}, u32[]{:S(2)}) collective-permute-start(bf16[2,64,1024]{2,1,0:T(8,128)(2,1)S(1)} %get-tuple-element.126), channel_id=1, source_target_pairs={{0,4},{4,0},{8,12},{12,8},{16,20},{20,16},{24,28},{28,24},{1,5},{5... | collective-permute-start | bytes 786440 | tf_op jit(solution)/shard_map/ppermute | solution.py:544
  4.7 26.0 %collective-permute-start.9 = (bf16[2,256,1024]{2,1,0:T(8,128)(2,1)}, bf16[2,256,1024]{2,1,0:T(8,128)(2,1)}, u32[]{:S(2)}, u32[]{:S(2)}) collective-permute-start(bf16[2,256,1024]{2,1,0:T(8,128)(2,1)} %get-tuple-element.134), channel_id=1, source_target_pairs={{2,3},{1,2},{5,4},{6,5},{10,11},{9,10},{13,12},{14,13},{18,19},{17... | collective-permute-start | bytes 3145736 | tf_op jit(solution)/shard_map/ppermute | solution.py:540
  7.6 0.7 copy-start.1
  7.6 1.2 %copy-start.2 = (bf16[512,1024]{1,0:T(8,128)(2,1)S(1)}, bf16[512,1024]{1,0:T(8,128)(2,1)}, u32[]{:S(2)}) copy-start(bf16[512,1024]{1,0:T(8,128)(2,1)} %param.15) | copy-start | bytes 3145732
  8.9 10.2 %collective-permute-start = (bf16[2,64,1024]{2,1,0:T(8,128)(2,1)S(1)}, bf16[2,64,1024]{2,1,0:T(8,128)(2,1)}, u32[]{:S(2)}, u32[]{:S(2)}) collective-permute-start(bf16[2,64,1024]{2,1,0:T(8,128)(2,1)S(1)} %get-tuple-element.63), channel_id=1, source_target_pairs={{0,1},{3,2},{4,5},{7,6},{8,9},{11,10},{12,13},{15,14},{16,17},{19,... | collective-permute-start | bytes 786440 | tf_op jit(solution)/shard_map/cond/branch_1_fun/ppermute | solution.py:476
  19.0 58.3 %collective-permute-start.10 = (bf16[2,256,1024]{2,1,0:T(8,128)(2,1)S(1)}, bf16[2,256,1024]{2,1,0:T(8,128)(2,1)S(1)}, u32[]{:S(2)}, u32[]{:S(2)}) collective-permute-start(bf16[2,256,1024]{2,1,0:T(8,128)(2,1)S(1)} %get-tuple-element.144), channel_id=1, source_target_pairs={{0,1},{3,2},{4,5},{7,6},{8,9},{11,10},{12,13},{15,14},{16,17},{19,... | collective-permute-start | bytes 3145736 | tf_op jit(solution)/shard_map/ppermute | solution.py:553
  24.6 5.5 %collective-permute-start.1 = (bf16[2,64,1024]{2,1,0:T(8,128)(2,1)S(1)}, bf16[2,64,1024]{2,1,0:T(8,128)(2,1)S(1)}, u32[]{:S(2)}, u32[]{:S(2)}) collective-permute-start(bf16[2,64,1024]{2,1,0:T(8,128)(2,1)S(1)} %get-tuple-element.67.held_ref), channel_id=1, source_target_pairs={{1,2},{2,1},{5,6},{6,5},{9,10},{10,9},{13,14},{14,13},{17,18},{18,... | collective-permute-start | bytes 786440 | tf_op jit(solution)/shard_map/cond/branch_1_fun/ppermute | solution.py:451
  30.8 10.2 %collective-permute-start.6 = (bf16[2,64,1024]{2,1,0:T(8,128)(2,1)S(1)}, bf16[2,64,1024]{2,1,0:T(8,128)(2,1)S(1)}, u32[]{:S(2)}, u32[]{:S(2)}) collective-permute-start(bf16[2,64,1024]{2,1,0:T(8,128)(2,1)S(1)} %get-tuple-element.90.held_ref), channel_id=1, source_target_pairs={{2,3},{1,0},{6,7},{5,4},{10,11},{9,8},{14,15},{13,12},{18,19},{17,... | collective-permute-start | bytes 786440 | tf_op jit(solution)/shard_map/cond/branch_1_fun/ppermute | solution.py:506
  33.0 44.3 %collective-permute-start.7 = (bf16[2,256,1024]{2,1,0:T(8,128)(2,1)}, bf16[2,256,1024]{2,1,0:T(8,128)(2,1)}, u32[]{:S(2)}, u32[]{:S(2)}) collective-permute-start(bf16[2,256,1024]{2,1,0:T(8,128)(2,1)} %get-tuple-element.103), channel_id=1, source_target_pairs={{1,0},{2,1},{6,7},{5,6},{9,8},{10,9},{14,15},{13,14},{17,16},{18,1... | collective-permute-start | bytes 3145736 | tf_op jit(solution)/shard_map/cond/branch_1_fun/ppermute | solution.py:495
  41.6 6.4 %collective-permute-start.3 = (bf16[2,64,1024]{2,1,0:T(8,128)(2,1)S(1)}, bf16[2,64,1024]{2,1,0:T(8,128)(2,1)S(1)}, u32[]{:S(2)}, u32[]{:S(2)}) collective-permute-start(bf16[2,64,1024]{2,1,0:T(8,128)(2,1)S(1)} %get-tuple-element.78.first), channel_id=1, source_target_pairs={{0,8},{4,20},{8,0},{12,28},{16,24},{20,4},{24,16},{28,12},{1,9},{5... | collective-permute-start | bytes 786440 | tf_op jit(solution)/shard_map/cond/branch_1_fun/cond/branch_1_fun/ppermute | solution.py:515
  48.0 9.2 %collective-permute-start.4 = (bf16[2,128,1024]{2,1,0:T(8,128)(2,1)S(1)}, bf16[2,128,1024]{2,1,0:T(8,128)(2,1)S(1)}, u32[]{:S(2)}, u32[]{:S(2)}) collective-permute-start(bf16[2,128,1024]{2,1,0:T(8,128)(2,1)S(1)} %join_pieces.2.first), channel_id=1, source_target_pairs={{0,16},{4,12},{8,24},{12,4},{16,0},{20,28},{24,8},{28,20},{1,17},{... | collective-permute-start | bytes 1572872 | tf_op jit(solution)/shard_map/cond/branch_1_fun/cond/branch_1_fun/ppermute | solution.py:515
  57.3 20.0 %collective-permute-start.5 = (bf16[2,256,1024]{2,1,0:T(8,128)(2,1)}, bf16[2,256,1024]{2,1,0:T(8,128)(2,1)}, u32[]{:S(2)}, u32[]{:S(2)}) collective-permute-start(bf16[2,256,1024]{2,1,0:T(8,128)(2,1)} %get-tuple-element.87), channel_id=1, source_target_pairs={{7,8},{8,7},{15,16},{16,15},{23,24},{24,23}} | collective-permute-start | bytes 3145736 | tf_op jit(solution)/shard_map/cond/branch_1_fun/cond/branch_1_fun/ppermute | solution.py:518
  62.0 2.9 %collective-permute-start.2 = (bf16[2,256,1024]{2,1,0:T(8,128)(2,1)}, bf16[2,256,1024]{2,1,0:T(8,128)(2,1)S(1)}, u32[]{:S(2)}, u32[]{:S(2)}) collective-permute-start(bf16[2,256,1024]{2,1,0:T(8,128)(2,1)} %get-tuple-element.76.rest_0_), channel_id=1, source_target_pairs={{0,4},{4,0},{8,12},{12,8},{16,20},{20,16},{24,28},{28,24},{1,5},{5... | collective-permute-start | bytes 3145736 | tf_op jit(solution)/shard_map/cond/branch_1_fun/cond/branch_1_fun/cond/branch_1_fun/ppermute | solution.py:529

commit v4 on v3

--- a/solution.py
+++ b/solution.py
@@ -160,10 +160,6 @@
     out_ref[...] = jnp.where(rule(lists_ref[0, 2 * BAND + 1]), got_ref[...], held_ref[...])
 
 
-def place_kernel(order_ref, place_ref):
-    place_ref[...] = place_rows(local_order(order_ref))
-
-
 def query_kernel(order_ref, q_ref, qs_ref, pick):
     @pl.when(pl.program_id(0) == 0)
     def _():
@@ -232,8 +228,8 @@
     new_ml_ref[...] = jnp.concatenate(peaks + totals, axis=0)
 
 
-def finish_kernel(lists_ref, place_ref, qs_ref, acc_ref, ml_ref, *rest):
-    next_kv, second_kv, odd_kv, out_ref, attended, halos, arrived = rest
+def finish_kernel(lists_ref, order_ref, qs_ref, acc_ref, ml_ref, *rest):
+    next_kv, second_kv, odd_kv, out_ref, attended, halos, place, arrived = rest
     count = qs_ref.shape[0]
     here, end = lax.axis_index("grp"), lax.axis_size("grp") - 1
     at_end = (here == 0) | (here == end)
@@ -264,6 +260,8 @@
                 def _():
                     for copy in copies_of(side, source, block):
                         copy.start()
+
+        place[...] = place_rows(local_order(order_ref))
 
     def wait_for(side):
         for block in range(blocks):
@@ -308,7 +306,7 @@
             total = ml_ref[PAIR_HEADS + at : PAIR_HEADS + at + 1, left]
             attended[cols, left] = (acc_ref[cols, left] / total).astype(jnp.bfloat16)
 
-    out_ref[...] = mm_nt(place_ref[...], attended[...]).astype(jnp.bfloat16)
+    out_ref[...] = mm_nt(place[...], attended[...]).astype(jnp.bfloat16)
 
 
 def join_kernel(first, second, joined):
@@ -488,10 +486,6 @@
         return relay(piece, [across_round]), own
 
     def outward_stage(piece, outward, second_out, queries, own, near_kv):
-        place = call(
-            place_kernel, "place_rows", [VMEM], VMEM, bf16((row_count, row_count)), cost=busy
-        )(order)
-        place, second_out = tie((place, second_out))
         second_kv = lax.ppermute(second_out, ("blk", "grp"), exchange(1))
         own = call(
             near_kernel,
@@ -506,7 +500,7 @@
         got = lax.ppermute(piece, "grp", outward_rounds[-1][0])
         piece = take(outward_rounds[-1][1], got, piece, flops=LONG)
         states, odd_kv = stage(plane_stage, piece, outward, queries, own)
-        return states, place, second_kv, odd_kv
+        return states, second_kv, odd_kv
 
     def plane_stage(piece, outward, queries, own):
         for step in range(2):
@@ -554,20 +548,21 @@
     piece = take(inward_rounds[-1][1], got, piece)
     piece, own = stage(across_stage, piece, kv, queries)
     piece, near_kv = tie((piece, near_kv))
-    states, place, second_kv, odd_kv = stage(outward_stage, piece, outward, second_out, queries, own, near_kv)
+    states, second_kv, odd_kv = stage(outward_stage, piece, outward, second_out, queries, own, near_kv)
     return call(
         finish_kernel,
         "attend_last",
-        [SMEM, whole_block(row_count, row_count), queries_block] + state_blocks + [ANY] * 3,
+        [SMEM, whole_block(1, row_count), queries_block] + state_blocks + [ANY] * 3,
         queries_block,
         bf16((row_count, feature_count)),
         [
             pltpu.VMEM((PAIR, row_count), jnp.bfloat16),
             pltpu.VMEM((2, 2, HALO, feature_count), jnp.bfloat16),
+            pltpu.VMEM((row_count, row_count), jnp.bfloat16),
             pltpu.SemaphoreType.DMA((2, 2, grid[0])),
         ],
         grid=grid,
-    )(tile_lists, place, queries, *states, next_kv, second_kv, odd_kv)
+    )(tile_lists, order, queries, *states, next_kv, second_kv, odd_kv)
 
 
 def solution(mesh):

time: 85.3 us -> 84.9 us (level)
  Pallas kernels: 32.1 us -> 30.8 us
  waiting for transfers between devices: 28.4 us -> 29.3 us
    pallas_call x2 -> x1, Pallas kernels: 8.53 us -> 7.21 us  [body(): call(finish_kernel, 'attend_last', [SMEM, whole_block(1, row_count), quer...]
    ppermute x1, waiting for transfers between devices: 4.05 us -> 4.94 us  [outward_stage(): got = lax.ppermute(piece, 'grp', outward_rounds[-1][0])]
  transfers between devices with their start and end apart: 11 -> 11, of which waited for: 6 -> 6; matrix products, arithmetic and copies ran while one was open for 1% -> 1% of each run, Pallas kernels for 23% -> 22%
where the time goes in v4:
time: 84.9 us; the launch traced here: 84.5 us
  Pallas kernels  30.8 us (36%)
  waiting for transfers between devices  29.3 us (35%)
  starting transfers between devices  22.4 us (26%)
  local copies, waits for them, and re-layouts  1.21 us (1%)
    ppermute x2, waiting for transfers between devices, plane_stage(): got = lax.ppermute(piece, 'blk', links)  13.5 us
    pallas_call x1, Pallas kernels, body(): call(finish_kernel, 'attend_last', [SMEM, whole_block(1, row_count), quer...  7.21 us
    ppermute x1, starting transfers between devices, inward_stage(): return (lax.ppermute(piece, 'grp', inward_rounds[-1][0]), queries)  7.02 us
    ppermute x1, waiting for transfers between devices, plane_stage(): odd_kv = lax.ppermute(outward, ('blk', 'grp'), wraps[1])  6.76 us
    pallas_call x1, Pallas kernels, global_stage(): call(global_kernel, 'attend_global', [SMEM, queries_block] + state_blocks...  5.68 us
    ppermute x1, waiting for transfers between devices, outward_stage(): got = lax.ppermute(piece, 'grp', outward_rounds[-1][0])  4.94 us
    pallas_call x1, Pallas kernels, across_stage(): call(own_kernel, 'attend_own', [SMEM, queries_block, column_block(2, row_...  4.8 us
    pallas_call x1, Pallas kernels, body(): call(sort_kernel, 'sort_keys_values', [HBM] * 4, [ANY] * (5 + part), [bf1...  4.64 us
  transfers between devices with their start and end apart: 11, of which 6 were waited for; matrix products, arithmetic and copies ran while one was open for 1% of the time, Pallas kernels for 22%

profile of v4, /device:TPU:4, one launch (start us, length us, event | category | flops | bytes accessed | tf_op | source)
XLA Modules:
  0.0 84.5 jit_solution(10412591450444073171)
XLA Ops:
  0.0 4.6 %sort_keys_values.1 = (bf16[2,512,1024]{2,1,0:T(8,128)(2,1)}, bf16[2,256,1024]{2,1,0:T(8,128)(2,1)}, bf16[2,256,1024]{2,1,0:T(8,128)(2,1)S(1)}, bf16[2,256,1024]...) custom-call(s32[4,9]{1,0:T(4,128)} %lists_ref.5, ...), custom_call_target="tpu_custom_call" | custom-call | tf_op jit(solution)/shard_map/sort_keys_values/pallas_call | solution.py:388
  4.7 1.6 %collective-permute-start.9 = (bf16[2,256,1024]{2,1,0:T(8,128)(2,1)}, bf16[2,256,1024]{2,1,0:T(8,128)(2,1)}, u32[]{:S(2)}, u32[]{:S(2)}) collective-permute-start(bf16[2,256,1024]{2,1,0:T(8,128)(2,1)} %get-tuple-element.128), channel_id=1, source_target_pairs={{2,3},{1,2},{5,4},{6,5},{10,11},{9,10},{13,12},{14,13},{18,19},{17... | collective-permute-start | bytes 3145736 | tf_op jit(solution)/shard_map/ppermute | solution.py:534
  6.4 0.6 slice.3
  7.6 0.6 select_piece.6.held_ref
  8.9 10.2 %conditional.5 = (bf16[2,64,1024]{2,1,0:T(8,128)(2,1)}, bf16[512,1024]{1,0:T(8,128)(2,1)}) conditional(s32[]{:T(128)} %convert_element_type.11, () %tuple.47, (bf16[2,64,1024]{2,1,0:T(8,128)(2,1)S(1)}, s32[1,512]{1,0:T(1,128)S(1)}, bf16[512,1024]{1,0:T(8,128)(2,1)S(1)}) %tuple.70), branch_computations={%region_0.0_spmd, %region_1.0_spmd} | conditional | flops 20000000000 | bytes 20001048576 | solution.py:445
  8.9 7.0 %collective-permute-start = (bf16[2,64,1024]{2,1,0:T(8,128)(2,1)S(1)}, bf16[2,64,1024]{2,1,0:T(8,128)(2,1)}, u32[]{:S(2)}, u32[]{:S(2)}) collective-permute-start(bf16[2,64,1024]{2,1,0:T(8,128)(2,1)S(1)} %get-tuple-element.61), channel_id=1, source_target_pairs={{0,1},{3,2},{4,5},{7,6},{8,9},{11,10},{12,13},{15,14},{16,17},{19,... | collective-permute-start | bytes 786440 | tf_op jit(solution)/shard_map/cond/branch_1_fun/ppermute | solution.py:474
  15.9 2.0 %sort_queries.1 = bf16[512,1024]{1,0:T(8,128)(2,1)} custom-call(s32[1,512]{1,0:T(1,128)S(1)} %get-tuple-element.62.order_ref, bf16[512,1024]{1,0:T(8,128)(2,1)S(1)} %get-tuple-element.141.q_ref), custom_call_target="tpu_custom_call" | custom-call | flops 20000000000 | bytes 20000000000 | tf_op jit(solution)/shard_map/cond/branch_1_fun/sort_queries/pallas_call | solution.py:464
  17.9 1.2 %collective-permute-done = bf16[2,64,1024]{2,1,0:T(8,128)(2,1)} collective-permute-done((bf16[2,64,1024]{2,1,0:T(8,128)(2,1)S(1)}, bf16[2,64,1024]{2,1,0:T(8,128)(2,1)}, u32[]{:S(2)}, u32[]{:S(2)}) %collective-permute-start) | collective-permute-done | bytes 262176 | tf_op jit(solution)/shard_map/cond/branch_1_fun/ppermute | solution.py:474
  19.0 4.5 %collective-permute-start.10 = (bf16[2,256,1024]{2,1,0:T(8,128)(2,1)S(1)}, bf16[2,256,1024]{2,1,0:T(8,128)(2,1)S(1)}, u32[]{:S(2)}, u32[]{:S(2)}) collective-permute-start(bf16[2,256,1024]{2,1,0:T(8,128)(2,1)S(1)} %get-tuple-element.137), channel_id=1, source_target_pairs={{0,1},{3,2},{4,5},{7,6},{8,9},{11,10},{12,13},{15,14},{16,17},{19,... | collective-permute-start | bytes 3145736 | tf_op jit(solution)/shard_map/ppermute | solution.py:547
  23.6 1.0 %select_piece.7 = bf16[2,64,1024]{2,1,0:T(8,128)(2,1)S(1)} custom-call(s32[4,9]{1,0:T(4,128)S(1)} %copy-done, bf16[2,64,1024]{2,1,0:T(8,128)(2,1)} %get-tuple-element.125.got_ref, bf16[2,64,1024]{2,1,0:T(8,128)(2,1)S(1)} %select_piece.6.held_ref), custom_call_target="tpu_custom_call" | custom-call | flops 1 | bytes 1 | tf_op jit(solution)/shard_map/select_piece/pallas_call | solution.py:412
  24.6 6.1 %conditional.6 = (bf16[2,64,1024]{2,1,0:T(8,128)(2,1)S(1)}, f32[1024,512]{1,0:T(8,128)S(1)}, f32[16,512]{1,0:T(8,128)S(1)}) conditional(s32[]{:T(128)} %convert_element_type.11, () %tuple.50, (bf16[2,64,1024]{2,1,0:T(8,128)(2,1)S(1)}, s32[4,9]{1,0:T(4,128)S(1)}, bf16[512,1024]{1,0:T(8,128)(2,1)}, bf16[2,512,1024]{2,1,0:T(8,128)(2,1)}) %tuple.67), branch_computations={%region_2.0_spmd, %region_3.0_spmd} | conditional | flops 20000000000 | bytes 20001048576 | solution.py:445
  24.6 0.7 collective-permute-start.1
  25.3 4.8 %attend_own.1 = (f32[1024,512]{1,0:T(8,128)S(1)}, f32[16,512]{1,0:T(8,128)S(1)}) custom-call(s32[4,9]{1,0:T(4,128)S(1)} %get-tuple-element.64.lists_ref, bf16[512,1024]{1,0:T(8,128)(2,1)} %get-tuple-element.66.qs_ref, bf16[2,512,1024]{2,1,0:T(8,128)(2,1)} %get-tuple-element.67.kv_ref), custom_call_target="tpu_custom_call" | custom-call | flops 20000000000 | bytes 20000000000 | tf_op jit(solution)/shard_map/cond/branch_1_fun/attend_own/pallas_call | solution.py:477
  30.1 0.6 select_piece.4
  30.7 46.6 %conditional.7 = (f32[1024,512]{1,0:T(8,128)}, f32[16,512]{1,0:T(8,128)}, bf16[2,256,1024]{2,1,0:T(8,128)(2,1)}, bf16[2,256,1024]{2,1,0:T(8,128)(2,1)}) conditional(s32[]{:T(128)} %convert_element_type.11, () %tuple.49, (pred[]{:T(512)}, bf16[2,64,1024]{2,1,0:T(8,128)(2,1)S(1)}, s32[4,9]{1,0:T(4,128)S(1)}, bf16[512,1024]{1,0:T(8,128)(2,1)}, ...), branch_computations={%region_4.0_spmd, %region_5.0_spmd} | conditional | flops 60000002048 | bytes 60016779264 | solution.py:445
  30.8 1.3 %collective-permute-start.6 = (bf16[2,64,1024]{2,1,0:T(8,128)(2,1)S(1)}, bf16[2,64,1024]{2,1,0:T(8,128)(2,1)S(1)}, u32[]{:S(2)}, u32[]{:S(2)}) collective-permute-start(bf16[2,64,1024]{2,1,0:T(8,128)(2,1)S(1)} %get-tuple-element.88.held_ref), channel_id=1, source_target_pairs={{2,3},{1,0},{6,7},{5,4},{10,11},{9,8},{14,15},{13,12},{18,19},{17,... | collective-permute-start | bytes 786440 | tf_op jit(solution)/shard_map/cond/branch_1_fun/ppermute | solution.py:500
  32.1 1.3 %collective-permute-start.7 = (bf16[2,256,1024]{2,1,0:T(8,128)(2,1)}, bf16[2,256,1024]{2,1,0:T(8,128)(2,1)}, u32[]{:S(2)}, u32[]{:S(2)}) collective-permute-start(bf16[2,256,1024]{2,1,0:T(8,128)(2,1)} %get-tuple-element.98), channel_id=1, source_target_pairs={{1,0},{2,1},{6,7},{5,6},{9,8},{10,9},{14,15},{13,14},{17,16},{18,1... | collective-permute-start | bytes 3145736 | tf_op jit(solution)/shard_map/cond/branch_1_fun/ppermute | solution.py:489
  33.4 2.6 %attend_near.1 = (f32[1024,512]{1,0:T(8,128)}, f32[16,512]{1,0:T(8,128)S(1)}) custom-call(s32[4,9]{1,0:T(4,128)S(1)} %get-tuple-element.87.lists_ref, bf16[512,1024]{1,0:T(8,128)(2,1)} %get-tuple-element.90.qs_ref, bf16[2,256,1024]{2,1,0:T(8,128)(2,1)} %get-tuple-element.91.near_kv, f32[1024,512]{1,0:T(8,128)S(1)} %get-tuple-element.92.acc_ref, ...), custom_call_target="tpu_custom_call" | custom-call | flops 20000000000 | bytes 20000000000 | tf_op jit(solution)/shard_map/cond/branch_1_fun/attend_near/pallas_call | solution.py:490
  36.0 4.9 %collective-permute-done.6.got_ref = bf16[2,64,1024]{2,1,0:T(8,128)(2,1)S(1)} collective-permute-done((bf16[2,64,1024]{2,1,0:T(8,128)(2,1)S(1)}, bf16[2,64,1024]{2,1,0:T(8,128)(2,1)S(1)}, u32[]{:S(2)}, u32[]{:S(2)}) %collective-permute-start.6) | collective-permute-done | bytes 262176 | tf_op jit(solution)/shard_map/cond/branch_1_fun/ppermute | solution.py:500
  40.9 0.6 select_piece.5
  41.5 35.8 %conditional.1 = (f32[1024,512]{1,0:T(8,128)}, f32[16,512]{1,0:T(8,128)}, bf16[2,256,1024]{2,1,0:T(8,128)(2,1)}) conditional(s32[]{:T(128)} %convert_element_type.2, () %tuple.36, (pred[]{:T(512)}, bf16[2,64,1024]{2,1,0:T(8,128)(2,1)S(1)}, bf16[2,256,1024]{2,1,0:T(8,128)(2,1)}, s32[4,9]{1,0:T(4,128)S(1)}, bf16[512,1024]{1,0:T(8,128)(2,1)}, ...), branch_computations={%region_6.0_spmd, %region_7.0_spmd} | conditional | flops 20000000000 | bytes 20011534336 | solution.py:445
  41.6 1.6 %collective-permute-start.3 = (bf16[2,64,1024]{2,1,0:T(8,128)(2,1)S(1)}, bf16[2,64,1024]{2,1,0:T(8,128)(2,1)S(1)}, u32[]{:S(2)}, u32[]{:S(2)}) collective-permute-start(bf16[2,64,1024]{2,1,0:T(8,128)(2,1)S(1)} %get-tuple-element.76.first), channel_id=1, source_target_pairs={{0,8},{4,20},{8,0},{12,28},{16,24},{20,4},{24,16},{28,12},{1,9},{5... | collective-permute-start | bytes 786440 | tf_op jit(solution)/shard_map/cond/branch_1_fun/cond/branch_1_fun/ppermute | solution.py:509
  43.1 4.9 %collective-permute-done.3.second = bf16[2,64,1024]{2,1,0:T(8,128)(2,1)S(1)} collective-permute-done((bf16[2,64,1024]{2,1,0:T(8,128)(2,1)S(1)}, bf16[2,64,1024]{2,1,0:T(8,128)(2,1)S(1)}, u32[]{:S(2)}, u32[]{:S(2)}) %collective-permute-start.3) | collective-permute-done | bytes 262176 | tf_op jit(solution)/shard_map/cond/branch_1_fun/cond/branch_1_fun/ppermute | solution.py:509
  48.0 0.6 collective-permute-start.4
  48.6 8.7 %collective-permute-done.4.second = bf16[2,128,1024]{2,1,0:T(8,128)(2,1)S(1)} collective-permute-done((bf16[2,128,1024]{2,1,0:T(8,128)(2,1)S(1)}, bf16[2,128,1024]{2,1,0:T(8,128)(2,1)S(1)}, u32[]{:S(2)}, u32[]{:S(2)}) %collective-permute-start.4) | collective-permute-done | bytes 524320 | tf_op jit(solution)/shard_map/cond/branch_1_fun/cond/branch_1_fun/ppermute | solution.py:509
  57.3 3.7 %collective-permute-start.5 = (bf16[2,256,1024]{2,1,0:T(8,128)(2,1)}, bf16[2,256,1024]{2,1,0:T(8,128)(2,1)}, u32[]{:S(2)}, u32[]{:S(2)}) collective-permute-start(bf16[2,256,1024]{2,1,0:T(8,128)(2,1)} %get-tuple-element.85), channel_id=1, source_target_pairs={{7,8},{8,7},{15,16},{16,15},{23,24},{24,23}} | collective-permute-start | bytes 3145736 | tf_op jit(solution)/shard_map/cond/branch_1_fun/cond/branch_1_fun/ppermute | solution.py:512
  61.0 1.0 %join_pieces.3 = bf16[2,256,1024]{2,1,0:T(8,128)(2,1)} custom-call(bf16[2,128,1024]{2,1,0:T(8,128)(2,1)S(1)} %join_pieces.2.first, bf16[2,128,1024]{2,1,0:T(8,128)(2,1)S(1)} %collective-permute-done.4.second), custom_call_target="tpu_custom_call" | custom-call | flops 20000000000 | bytes 20000000000 | tf_op jit(solution)/shard_map/cond/branch_1_fun/cond/branch_1_fun/join_pieces/pallas_call | solution.py:516
  62.0 8.6 %conditional = ((f32[1024,512]{1,0:T(8,128)}, f32[16,512]{1,0:T(8,128)})) conditional(s32[]{:T(128)} %convert_element_type.1, () %tuple.32, (bf16[2,256,1024]{2,1,0:T(8,128)(2,1)}, s32[4,9]{1,0:T(4,128)S(1)}, bf16[512,1024]{1,0:T(8,128)(2,1)}, f32[1024,512]{1,0:T(8,128)}, f32[16,512]{1,0:T(8,128)S(1)}) %tuple.34), branch_computations={%region_8.0_spmd, %region_9.0_spmd} | conditional | flops 1 | bytes 4194353 | solution.py:445
  62.0 2.9 %collective-permute-done.2.rest_1_ = bf16[2,256,1024]{2,1,0:T(8,128)(2,1)S(1)} collective-permute-done((bf16[2,256,1024]{2,1,0:T(8,128)(2,1)}, bf16[2,256,1024]{2,1,0:T(8,128)(2,1)S(1)}, u32[]{:S(2)}, u32[]{:S(2)}) %collective-permute-start.2) | collective-permute-done | bytes 1048608 | tf_op jit(solution)/shard_map/cond/branch_1_fun/cond/branch_1_fun/cond/branch_1_fun/ppermute | solution.py:523
  64.9 5.7 %attend_global.1 = (f32[1024,512]{1,0:T(8,128)}, f32[16,512]{1,0:T(8,128)}) custom-call(s32[4,9]{1,0:T(4,128)S(1)} %get-tuple-element.70.lists_ref, bf16[512,1024]{1,0:T(8,128)(2,1)} %get-tuple-element.71.qs_ref, f32[1024,512]{1,0:T(8,128)} %get-tuple-element.72.acc_ref, f32[16,512]{1,0:T(8,128)S(1)} %get-tuple-element.73.ml_ref, ...), custom_call_target="tpu_custom_call" | custom-call | flops 1 | bytes 1 | tf_op jit(solution)/shard_map/cond/branch_1_fun/cond/branch_1_fun/cond/branch_1_fun/attend_global/pallas_call | solution.py:524
  70.6 6.8 %collective-permute-done.5 = bf16[2,256,1024]{2,1,0:T(8,128)(2,1)} collective-permute-done((bf16[2,256,1024]{2,1,0:T(8,128)(2,1)}, bf16[2,256,1024]{2,1,0:T(8,128)(2,1)}, u32[]{:S(2)}, u32[]{:S(2)}) %collective-permute-start.5) | collective-permute-done | bytes 1048608 | tf_op jit(solution)/shard_map/cond/branch_1_fun/cond/branch_1_fun/ppermute | solution.py:512
  77.3 7.2 %attend_last.1 = bf16[512,1024]{1,0:T(8,128)(2,1)} custom-call(s32[4,9]{1,0:T(4,128)S(1)} %copy-done, s32[1,512]{1,0:T(1,128)S(1)} %bitcast.4, bf16[512,1024]{1,0:T(8,128)(2,1)} %get-tuple-element.122.qs_ref, f32[1024,512]{1,0:T(8,128)} %get-tuple-element.135.acc_ref, f32[16,512]{1,0:T(8,128)} %get-tuple-element.136.ml_ref, ...), custom_call_target="tpu_custom_call" | custom-call | tf_op jit(solution)/shard_map/attend_last/pallas_call | solution.py:552
  (14 shorter events, 0.7 us)
Async XLA Ops:
  0.0 6.4 %copy-start = (s32[4,9]{1,0:T(4,128)S(1)}, s32[4,9]{1,0:T(4,128)}, u32[]{:S(2)}) copy-start(s32[4,9]{1,0:T(4,128)} %lists_ref.5) | copy-start | bytes 436
  4.7 3.0 %collective-permute-start.8 = (bf16[2,64,1024]{2,1,0:T(8,128)(2,1)S(1)}, bf16[2,64,1024]{2,1,0:T(8,128)(2,1)S(1)}, u32[]{:S(2)}, u32[]{:S(2)}) collective-permute-start(bf16[2,64,1024]{2,1,0:T(8,128)(2,1)S(1)} %get-tuple-element.120), channel_id=1, source_target_pairs={{0,4},{4,0},{8,12},{12,8},{16,20},{20,16},{24,28},{28,24},{1,5},{5... | collective-permute-start | bytes 786440 | tf_op jit(solution)/shard_map/ppermute | solution.py:538
  4.7 26.0 %collective-permute-start.9 = (bf16[2,256,1024]{2,1,0:T(8,128)(2,1)}, bf16[2,256,1024]{2,1,0:T(8,128)(2,1)}, u32[]{:S(2)}, u32[]{:S(2)}) collective-permute-start(bf16[2,256,1024]{2,1,0:T(8,128)(2,1)} %get-tuple-element.128), channel_id=1, source_target_pairs={{2,3},{1,2},{5,4},{6,5},{10,11},{9,10},{13,12},{14,13},{18,19},{17... | collective-permute-start | bytes 3145736 | tf_op jit(solution)/shard_map/ppermute | solution.py:534
  7.6 0.7 copy-start.1
  7.6 1.2 %copy-start.2 = (bf16[512,1024]{1,0:T(8,128)(2,1)S(1)}, bf16[512,1024]{1,0:T(8,128)(2,1)}, u32[]{:S(2)}) copy-start(bf16[512,1024]{1,0:T(8,128)(2,1)} %param.15) | copy-start | bytes 3145732
  8.9 10.2 %collective-permute-start = (bf16[2,64,1024]{2,1,0:T(8,128)(2,1)S(1)}, bf16[2,64,1024]{2,1,0:T(8,128)(2,1)}, u32[]{:S(2)}, u32[]{:S(2)}) collective-permute-start(bf16[2,64,1024]{2,1,0:T(8,128)(2,1)S(1)} %get-tuple-element.61), channel_id=1, source_target_pairs={{0,1},{3,2},{4,5},{7,6},{8,9},{11,10},{12,13},{15,14},{16,17},{19,... | collective-permute-start | bytes 786440 | tf_op jit(solution)/shard_map/cond/branch_1_fun/ppermute | solution.py:474
  19.0 58.3 %collective-permute-start.10 = (bf16[2,256,1024]{2,1,0:T(8,128)(2,1)S(1)}, bf16[2,256,1024]{2,1,0:T(8,128)(2,1)S(1)}, u32[]{:S(2)}, u32[]{:S(2)}) collective-permute-start(bf16[2,256,1024]{2,1,0:T(8,128)(2,1)S(1)} %get-tuple-element.137), channel_id=1, source_target_pairs={{0,1},{3,2},{4,5},{7,6},{8,9},{11,10},{12,13},{15,14},{16,17},{19,... | collective-permute-start | bytes 3145736 | tf_op jit(solution)/shard_map/ppermute | solution.py:547
  24.6 5.5 %collective-permute-start.1 = (bf16[2,64,1024]{2,1,0:T(8,128)(2,1)S(1)}, bf16[2,64,1024]{2,1,0:T(8,128)(2,1)S(1)}, u32[]{:S(2)}, u32[]{:S(2)}) collective-permute-start(bf16[2,64,1024]{2,1,0:T(8,128)(2,1)S(1)} %get-tuple-element.65.held_ref), channel_id=1, source_target_pairs={{1,2},{2,1},{5,6},{6,5},{9,10},{10,9},{13,14},{14,13},{17,18},{18,... | collective-permute-start | bytes 786440 | tf_op jit(solution)/shard_map/cond/branch_1_fun/ppermute | solution.py:449
  30.8 10.2 %collective-permute-start.6 = (bf16[2,64,1024]{2,1,0:T(8,128)(2,1)S(1)}, bf16[2,64,1024]{2,1,0:T(8,128)(2,1)S(1)}, u32[]{:S(2)}, u32[]{:S(2)}) collective-permute-start(bf16[2,64,1024]{2,1,0:T(8,128)(2,1)S(1)} %get-tuple-element.88.held_ref), channel_id=1, source_target_pairs={{2,3},{1,0},{6,7},{5,4},{10,11},{9,8},{14,15},{13,12},{18,19},{17,... | collective-permute-start | bytes 786440 | tf_op jit(solution)/shard_map/cond/branch_1_fun/ppermute | solution.py:500
  32.1 45.3 %collective-permute-start.7 = (bf16[2,256,1024]{2,1,0:T(8,128)(2,1)}, bf16[2,256,1024]{2,1,0:T(8,128)(2,1)}, u32[]{:S(2)}, u32[]{:S(2)}) collective-permute-start(bf16[2,256,1024]{2,1,0:T(8,128)(2,1)} %get-tuple-element.98), channel_id=1, source_target_pairs={{1,0},{2,1},{6,7},{5,6},{9,8},{10,9},{14,15},{13,14},{17,16},{18,1... | collective-permute-start | bytes 3145736 | tf_op jit(solution)/shard_map/cond/branch_1_fun/ppermute | solution.py:489
  41.6 6.4 %collective-permute-start.3 = (bf16[2,64,1024]{2,1,0:T(8,128)(2,1)S(1)}, bf16[2,64,1024]{2,1,0:T(8,128)(2,1)S(1)}, u32[]{:S(2)}, u32[]{:S(2)}) collective-permute-start(bf16[2,64,1024]{2,1,0:T(8,128)(2,1)S(1)} %get-tuple-element.76.first), channel_id=1, source_target_pairs={{0,8},{4,20},{8,0},{12,28},{16,24},{20,4},{24,16},{28,12},{1,9},{5... | collective-permute-start | bytes 786440 | tf_op jit(solution)/shard_map/cond/branch_1_fun/cond/branch_1_fun/ppermute | solution.py:509
  48.0 9.2 %collective-permute-start.4 = (bf16[2,128,1024]{2,1,0:T(8,128)(2,1)S(1)}, bf16[2,128,1024]{2,1,0:T(8,128)(2,1)S(1)}, u32[]{:S(2)}, u32[]{:S(2)}) collective-permute-start(bf16[2,128,1024]{2,1,0:T(8,128)(2,1)S(1)} %join_pieces.2.first), channel_id=1, source_target_pairs={{0,16},{4,12},{8,24},{12,4},{16,0},{20,28},{24,8},{28,20},{1,17},{... | collective-permute-start | bytes 1572872 | tf_op jit(solution)/shard_map/cond/branch_1_fun/cond/branch_1_fun/ppermute | solution.py:509
  57.3 20.0 %collective-permute-start.5 = (bf16[2,256,1024]{2,1,0:T(8,128)(2,1)}, bf16[2,256,1024]{2,1,0:T(8,128)(2,1)}, u32[]{:S(2)}, u32[]{:S(2)}) collective-permute-start(bf16[2,256,1024]{2,1,0:T(8,128)(2,1)} %get-tuple-element.85), channel_id=1, source_target_pairs={{7,8},{8,7},{15,16},{16,15},{23,24},{24,23}} | collective-permute-start | bytes 3145736 | tf_op jit(solution)/shard_map/cond/branch_1_fun/cond/branch_1_fun/ppermute | solution.py:512
  62.0 2.9 %collective-permute-start.2 = (bf16[2,256,1024]{2,1,0:T(8,128)(2,1)}, bf16[2,256,1024]{2,1,0:T(8,128)(2,1)S(1)}, u32[]{:S(2)}, u32[]{:S(2)}) collective-permute-start(bf16[2,256,1024]{2,1,0:T(8,128)(2,1)} %get-tuple-element.74.rest_0_), channel_id=1, source_target_pairs={{0,4},{4,0},{8,12},{12,8},{16,20},{20,16},{24,28},{28,24},{1,5},{5... | collective-permute-start | bytes 3145736 | tf_op jit(solution)/shard_map/cond/branch_1_fun/cond/branch_1_fun/cond/branch_1_fun/ppermute | solution.py:523
